TPU v7x, 128 devices: a whole 4x4x4 slice. The times are simulated.
128 devices in a mesh: ctx: 16 (over z, y), exp: 8 (over x, core).
Axes of the slice: x: 4, y: 4, z: 4, core: 2. Of those that a mesh axis runs over, the one named last changes fastest.
Arguments:
- block_in: bfloat16 [8, 2048, 768], P('exp', 'ctx'), may hold values from -6 to 6
- attn_gain: bfloat16 [768], P('exp'), may hold values from 0.5 to 1.5
- moe_gain: bfloat16 [768], P('exp'), may hold values from 0.5 to 1.5
- query_key_value_weight: bfloat16 [768, 2304], P('exp'), may hold values from -0.21875 to 0.21875
- output_matrix: bfloat16 [768, 768], P('exp'), may hold values from -3.5 to 3.5
- routing_weight: bfloat16 [768, 8], P('exp'), may hold values from -0.15625 to 0.15625
- bias_table: bfloat16 [32, 12], P('exp'), may hold values from -4 to 4
- up_weight: bfloat16 [8, 3072, 768], P('exp', 'ctx'), may hold values from -0.21875 to 0.21875
- down_weight: bfloat16 [8, 3072, 768], P('exp', 'ctx'), may hold values from -0.109375 to 0.109375
- routes: int32 [8, 2048, 2], P('exp', 'ctx'), may hold values from 0 to 7, all different within a row; in each aligned block of 128 rows (0 to 127, 128 to 255, ..., all dimensions but the last counted through in order) at most 64 rows name the same one
- doc_lengths: int32 [8, 4], P('exp'), may hold values from 1 to 2045, as said below
- cotangent: bfloat16 [8, 2048, 768], P('exp', 'ctx'), may hold values from -6 to 6
Outputs:
- block_out: bfloat16 [8, 2048, 768], P('exp', 'ctx')
- grad_in: float32 [8, 2048, 768], P('exp', 'ctx')
- grad_attn_gain: float32 [768], P('exp')
- grad_moe_gain: float32 [768], P('exp')
- grad_qkv: float32 [768, 2304], P('exp')
- grad_out_weight: float32 [768, 768], P('exp')
- grad_router: float32 [768, 8], P('exp')
- grad_bias_table: float32 [32, 12], P('exp')
- grad_up: float32 [8, 3072, 768], P('exp', 'ctx')
- grad_down: float32 [8, 3072, 768], P('exp', 'ctx')
Inputs may be any that keep to these rules, and one draw needn't show every extreme that they name: `routes`: A token's two experts differ. In the 128 tokens of one device no expert is named more than 64 times; in the rows of some devices one expert is named exactly 64 times. `doc_lengths`: each row holds 4 lengths that sum to 2048; the second document starts within the sequence's first 128 positions and ends within its last 128.
All inputs are finite; a program needn't handle non-finite values.
Results may differ from a plain program's by a relative error of at most 0.028.
Values may be sent and summed in bfloat16 or wider, within the bound.
A program may use at most 256 MiB of HBM per device.

v0:
```python
import functools
import math

import jax
import jax.numpy as jnp
import numpy as np
from jax import lax
from jax.experimental import pallas as pl
from jax.experimental.pallas import tpu as pltpu
from jax.sharding import PartitionSpec as P

MAXD = 128
BLOCK = 256
MESH = pl.DeviceIdType.MESH
VMEM_BYTES = 40 * 1024 * 1024

epsilon = 1e-06
masked_score = -1e30


def bucket_thresholds(buckets, reach_len):
    exact_part = buckets // 2
    spread_part = buckets - exact_part
    return [
        int(math.ceil(exact_part * (reach_len / exact_part) ** (level / spread_part)))
        for level in range(1, spread_part)
    ]


def guarded(tests, action):
    tests = [t for t in tests if t is not None]
    if not tests:
        action()
    else:
        pl.when(functools.reduce(jnp.logical_and, tests))(action)


def greet(sizes, axes):
    barrier = pltpu.get_barrier_semaphore()
    total = 0
    for a in axes:
        me = lax.axis_index(a)
        for r in range(1, sizes[a]):
            peer = lax.rem(me + r, sizes[a])
            pl.semaphore_signal(barrier, inc=1, device_id={a: peer}, device_id_type=MESH)
            total += 1
    pl.semaphore_wait(barrier, total)


class Move:
    def __init__(self, sizes, axis, src, out, sems, split=False, senders=None, takers=None):
        self.n = sizes[axis]
        self.axis, self.src, self.out, self.split = axis, src, out, split
        self.send_sem, self.recv_sem, self.own_sem = sems
        self.senders, self.takers = senders or self.n, takers or self.n
        self.me = lax.axis_index(axis)

    def sends(self, device):
        return device < self.senders if self.senders < self.n else None

    def takes(self, device):
        return device < self.takers if self.takers < self.n else None

    def copy(self, r, peer, slot, piece):
        return pltpu.make_async_remote_copy(
            src_ref=self.src.at[piece] if self.split else self.src,
            dst_ref=self.out.at[slot],
            send_sem=self.send_sem.at[r],
            recv_sem=self.recv_sem.at[r],
            device_id={self.axis: peer},
            device_id_type=MESH,
        )

    def to(self, r):
        return lax.rem(self.me + r, self.n)

    def start(self, r):
        dst = self.to(r)
        guarded(
            [self.sends(self.me), self.takes(dst)],
            lambda: self.copy(r, dst, self.me, dst).start(),
        )

    def own(self):
        src = self.src.at[self.me] if self.split else self.src
        return pltpu.make_async_copy(src, self.out.at[self.me], self.own_sem)

    def start_own(self):
        guarded([self.sends(self.me), self.takes(self.me)], lambda: self.own().start())

    def wait(self):
        guarded([self.sends(self.me), self.takes(self.me)], lambda: self.own().wait())
        for r in range(1, self.n):
            src = lax.rem(self.me + self.n - r, self.n)
            guarded(
                [self.sends(src), self.takes(self.me)],
                lambda: self.copy(r, src, src, 0).wait_recv(),
            )

    def wait_sent(self):
        for r in range(1, self.n):
            dst = self.to(r)
            guarded(
                [self.sends(self.me), self.takes(dst)],
                lambda: self.copy(r, dst, self.me, dst).wait_send(),
            )


def start_all(moves):
    for r in range(1, max(m.n for m in moves)):
        for m in moves:
            if r < m.n:
                m.start(r)
    for m in moves:
        m.start_own()


class PairGather:
    def __init__(self, sizes, src, out, sems):
        self.n = sizes["exp"]
        self.src, self.out = src, out
        self.send_sem, self.recv_sem, self.own_sem = sems
        self.me = lax.axis_index("exp")
        core = lax.rem(self.me, 2)
        self.mate = self.me + 1 - 2 * core

    def copy(self, src, slot, k, peer):
        return pltpu.make_async_remote_copy(
            src_ref=src,
            dst_ref=self.out.at[slot],
            send_sem=self.send_sem.at[k],
            recv_sem=self.recv_sem.at[k],
            device_id={"exp": peer},
            device_id_type=MESH,
        )

    def own(self):
        return pltpu.make_async_copy(self.src, self.out.at[self.me], self.own_sem)

    def chips(self):
        return range(1, self.n // 2)

    def start(self):
        for r in self.chips():
            self.copy(self.src, self.me, r, lax.rem(self.me + 2 * r, self.n)).start()
        self.copy(self.src, self.me, 0, self.mate).start()
        self.own().start()

    def forward(self, r):
        slot = lax.rem(self.me + self.n - 2 * r, self.n)
        return self.copy(self.out.at[slot], slot, self.n // 2 + r, self.mate)

    def pass_on(self):
        for r in self.chips():
            slot = lax.rem(self.me + self.n - 2 * r, self.n)
            self.copy(self.src, slot, r, slot).wait_recv()
            self.forward(r).start()

    def finish(self):
        for r in self.chips():
            slot = lax.rem(self.mate + self.n - 2 * r, self.n)
            self.copy(self.src, slot, self.n // 2 + r, self.mate).wait_recv()
            self.forward(r).wait_send()
            self.copy(self.src, self.me, r, lax.rem(self.me + 2 * r, self.n)).wait_send()
        self.copy(self.src, self.mate, 0, self.mate).wait_recv()
        self.copy(self.src, self.me, 0, self.mate).wait_send()
        self.own().wait()


def move_sems(count):
    return [
        pltpu.SemaphoreType.DMA((count,)),
        pltpu.SemaphoreType.DMA((count,)),
        pltpu.SemaphoreType.DMA,
    ]


def any_space(count):
    return [pl.BlockSpec(memory_space=pl.ANY)] * count


def in_vmem(count):
    return [pl.BlockSpec(memory_space=pltpu.VMEM)] * count


def in_smem(count):
    return [pl.BlockSpec(memory_space=pltpu.SMEM)] * count


def remote_params(number, limit=VMEM_BYTES):
    return pltpu.CompilerParams(
        collective_id=number, has_side_effects=True, vmem_limit_bytes=limit
    )


def cost(flops, moved, special=0):
    return pl.CostEstimate(flops=flops, bytes_accessed=moved, transcendentals=special)


def gather_dense(sizes, weight, small):
    n = sizes["exp"]

    def kernel(w_ref, s_ref, w_out, s_out, *sems):
        greet(sizes, ["exp"])
        big = PairGather(sizes, w_ref, w_out, sems[:3])
        little = Move(sizes, "exp", s_ref, s_out, sems[3:])
        start_all([little])
        big.start()
        big.pass_on()
        big.finish()
        little.wait()
        little.wait_sent()

    return pl.pallas_call(
        kernel,
        out_shape=[jax.ShapeDtypeStruct((n,) + a.shape, a.dtype) for a in (weight, small)],
        in_specs=any_space(2),
        out_specs=any_space(2),
        scratch_shapes=move_sems(n) + move_sems(n),
        compiler_params=remote_params(1, 4 * 1024 * 1024),
        cost_estimate=cost(0, 40_000_000),
        name="gather_dense",
    )(weight, small)


def swap_experts(sizes, number, rows, values):
    n = sizes["exp"]

    def kernel(a_ref, b_ref, a_out, b_out, *sems):
        greet(sizes, ["exp"])
        one = Move(sizes, "exp", a_ref, a_out, sems[:3], split=True)
        two = Move(sizes, "exp", b_ref, b_out, sems[3:], split=True)
        start_all([two, one])
        for m in (two, one):
            m.wait()
        for m in (two, one):
            m.wait_sent()

    return pl.pallas_call(
        kernel,
        out_shape=[jax.ShapeDtypeStruct(a.shape, a.dtype) for a in (rows, values)],
        in_specs=any_space(2),
        out_specs=any_space(2),
        scratch_shapes=move_sems(n) + move_sems(n),
        compiler_params=remote_params(number, 4 * 1024 * 1024),
        cost_estimate=cost(0, 30_000_000),
        name=f"swap_experts_{number}",
    )(rows, values)


def dot_nt(left, right):
    return lax.dot_general(
        left, right, (((1,), (1,)), ((), ())), preferred_element_type=jnp.float32
    )


def dot_tn(left, right):
    return lax.dot_general(
        left, right, (((0,), (0,)), ((), ())), preferred_element_type=jnp.float32
    )


def dot_nn(left, right):
    return jnp.dot(left, right, preferred_element_type=jnp.float32)


def near_buckets(buckets, offset, rows, cols):
    key = lax.broadcasted_iota(jnp.int32, (rows, cols), 0)
    query = lax.broadcasted_iota(jnp.int32, (rows, cols), 1)
    distance = jnp.clip(query - key + offset, 0, MAXD)
    bucket = jnp.minimum(distance, buckets // 2)
    for level in bucket_thresholds(buckets, MAXD):
        bucket = bucket + (distance >= level).astype(jnp.int32)
    return bucket


def near_bias(table_ref, buckets, offset, rows, cols):
    bucket = near_buckets(buckets, offset, rows, cols)
    last = table_ref[buckets - 1]
    bias = jnp.zeros((rows, cols), jnp.float32)
    for b in range(buckets - 1):
        bias = jnp.where(bucket == b, table_ref[b] - last, bias)
    return bias


def first_keys(bounds_ref, start):
    query = start + lax.broadcasted_iota(jnp.int32, (1, BLOCK), 1)
    first = jnp.zeros((1, BLOCK), jnp.int32)
    for d in range(3):
        first = jnp.where(query >= bounds_ref[d], bounds_ref[d], first)
    return first


def block_scores(i, j, blocks, qt, k, diag_bias, side_bias, first):
    s = dot_nn(k, qt)
    half = BLOCK // 2
    if j == i:
        s = s + diag_bias
    elif j == i - 1:
        lower = jnp.concatenate([s[half:, :half] + side_bias, s[half:, half:]], axis=1)
        s = jnp.concatenate([s[:half], lower], axis=0)
    if j == i or j == 0 or i == blocks - 1:
        key = lax.broadcasted_iota(jnp.int32, (BLOCK, BLOCK), 0)
        keep = key + j * BLOCK >= first
        if j == i:
            keep = keep & (key <= lax.broadcasted_iota(jnp.int32, (BLOCK, BLOCK), 1))
        s = jnp.where(keep, s, masked_score)
    return s


def transposed(piece):
    return piece.astype(jnp.float32).T.astype(jnp.bfloat16)


def scaled_queries(qkv_ref, i, size):
    scale = 1.0 / math.sqrt(size)
    both = jnp.concatenate([qkv_ref[2 * i, :size, :], qkv_ref[2 * i + 1, :size, :]], axis=1)
    return (both * scale).astype(jnp.bfloat16)


def block_of(j):
    return slice(j * BLOCK, (j + 1) * BLOCK)


def forward_kernel(
    sizes,
    heads,
    buckets,
    qkv_in,
    proj_in,
    g_in,
    table_ref,
    bounds_ref,
    mixed_out,
    proj_out,
    g_out,
    qkv_ref,
    stat_ref,
    sent_ref,
    k_ref,
    vt_ref,
    diag_ref,
    side_ref,
    *sems,
):
    parts, _, rows = qkv_ref.shape
    size = sent_ref.shape[1]
    blocks = parts * rows // BLOCK
    half = BLOCK // 2
    greet(sizes, ["ctx", "exp"])
    arrive = Move(sizes, "ctx", qkv_in, qkv_ref, sems[0:3], split=True, takers=heads)
    back = Move(sizes, "ctx", sent_ref, mixed_out, sems[3:6], split=True, senders=heads)
    proj = PairGather(sizes, proj_in, proj_out, sems[6:9])
    grads = Move(sizes, "exp", g_in, g_out, sems[9:12], split=True)
    start_all([arrive])
    proj.start()
    start_all([grads])
    diag_ref[...] = near_bias(table_ref, buckets, 0, BLOCK, BLOCK)
    side_ref[...] = near_bias(table_ref, buckets, half, half, half)
    proj.pass_on()
    arrive.wait()

    @pl.when(lax.axis_index("ctx") < heads)
    def _():
        for c in range(parts):
            at = slice(c * rows, (c + 1) * rows)
            k_ref[at, :] = transposed(qkv_ref[c, size : 2 * size, :])
            vt_ref[:, at] = qkv_ref[c, 2 * size :, :]
        for i in range(blocks):
            qt = scaled_queries(qkv_ref, i, size)
            first = first_keys(bounds_ref, i * BLOCK)
            scores = []
            top = None
            for j in range(i + 1):
                s = block_scores(
                    i, j, blocks, qt, k_ref[block_of(j), :], diag_ref[...], side_ref[...], first
                )
                scores.append(s)
                here = jnp.max(s, axis=0, keepdims=True)
                top = here if top is None else jnp.maximum(top, here)
            total = jnp.zeros((1, BLOCK), jnp.float32)
            for j in range(i + 1):
                scores[j] = jnp.exp(scores[j] - top)
                total = total + jnp.sum(scores[j], axis=0, keepdims=True)
            inverse = 1.0 / total
            mixed = jnp.zeros((size, BLOCK), jnp.float32)
            for j in range(i + 1):
                probs = (scores[j] * inverse).astype(jnp.bfloat16)
                mixed = mixed + dot_nn(vt_ref[:, block_of(j)], probs)
            mixed = mixed.astype(jnp.bfloat16)
            sent_ref[2 * i] = mixed[:, :half]
            sent_ref[2 * i + 1] = mixed[:, half:]
            stat_ref[i : i + 1, :] = top + jnp.log(total)

    start_all([back])
    proj.finish()
    grads.wait()
    back.wait()
    for m in (arrive, back, grads):
        m.wait_sent()


def attention_forward(sizes, qkv, proj, g, table, bounds):
    n_ctx, n_exp = sizes["ctx"], sizes["exp"]
    heads, three, rows = qkv.shape
    size = three // 3
    buckets = table.shape[0]
    seq = n_ctx * rows
    low, full = jnp.bfloat16, jnp.float32
    assert 2 * rows == BLOCK
    return pl.pallas_call(
        functools.partial(forward_kernel, sizes, heads, buckets),
        out_shape=[
            jax.ShapeDtypeStruct((heads, size, rows), low),
            jax.ShapeDtypeStruct((n_exp,) + proj.shape, low),
            jax.ShapeDtypeStruct(g.shape, low),
            jax.ShapeDtypeStruct((n_ctx, three, rows), low),
            jax.ShapeDtypeStruct((seq // BLOCK, BLOCK), full),
        ],
        in_specs=any_space(3) + in_smem(2),
        out_specs=any_space(3) + in_vmem(2),
        scratch_shapes=[
            pltpu.VMEM((n_ctx, size, rows), low),
            pltpu.VMEM((seq, size), low),
            pltpu.VMEM((size, seq), low),
            pltpu.VMEM((BLOCK, BLOCK), full),
            pltpu.VMEM((BLOCK // 2, BLOCK // 2), full),
        ]
        + move_sems(n_ctx)
        + move_sems(n_ctx)
        + move_sems(n_exp)
        + move_sems(n_exp),
        compiler_params=remote_params(2),
        cost_estimate=cost(12_000_000_000, 50_000_000, 2_400_000),
        name="attention_forward",
    )(qkv, proj, g, table, bounds)


def backward_kernel(
    sizes,
    heads,
    buckets,
    do_in,
    out_in,
    terms_in,
    qkv_ref,
    stat_ref,
    table_ref,
    bounds_ref,
    grad_out,
    out_out,
    terms_out,
    grad_ref,
    bias_ref,
    do_ref,
    sent_ref,
    k_ref,
    v_ref,
    kt_ref,
    dq_ref,
    dk_ref,
    dv_ref,
    diag_ref,
    side_ref,
    diag_sum,
    side_sum,
    *sems,
):
    parts, three, rows = qkv_ref.shape
    size = three // 3
    blocks = parts * rows // BLOCK
    half = BLOCK // 2
    scale = 1.0 / math.sqrt(size)
    greet(sizes, ["ctx", "exp"])
    arrive = Move(sizes, "ctx", do_in, do_ref, sems[0:3], split=True, takers=heads)
    back = Move(sizes, "ctx", sent_ref, grad_out, sems[3:6], split=True, senders=heads)
    experts = Move(sizes, "exp", out_in, out_out, sems[6:9], split=True)
    terms = Move(sizes, "exp", terms_in, terms_out, sems[9:12], split=True)
    start_all([arrive])
    start_all([experts, terms])
    is_head = lax.axis_index("ctx") < heads

    @pl.when(is_head)
    def _():
        diag_ref[...] = near_bias(table_ref, buckets, 0, BLOCK, BLOCK)
        side_ref[...] = near_bias(table_ref, buckets, half, half, half)
        diag_sum[...] = jnp.zeros_like(diag_sum)
        side_sum[...] = jnp.zeros_like(side_sum)
        dk_ref[...] = jnp.zeros_like(dk_ref)
        dv_ref[...] = jnp.zeros_like(dv_ref)
        for c in range(parts):
            at = slice(c * rows, (c + 1) * rows)
            kt_ref[:, at] = qkv_ref[c, size : 2 * size, :]
            k_ref[at, :] = transposed(qkv_ref[c, size : 2 * size, :])
            v_ref[at, :] = transposed(qkv_ref[c, 2 * size :, :])

    arrive.wait()

    @pl.when(is_head)
    def _():
        far = jnp.zeros((1, BLOCK), jnp.float32)
        for i in range(blocks):
            qt = scaled_queries(qkv_ref, i, size)
            dot_ = jnp.concatenate([do_ref[2 * i], do_ref[2 * i + 1]], axis=1)
            first = first_keys(bounds_ref, i * BLOCK)
            stat = stat_ref[i : i + 1, :]
            probs, grads = [], []
            delta = jnp.zeros((1, BLOCK), jnp.float32)
            for j in range(i + 1):
                s = block_scores(
                    i, j, blocks, qt, k_ref[block_of(j), :], diag_ref[...], side_ref[...], first
                )
                p = jnp.exp(s - stat)
                dp = dot_nn(v_ref[block_of(j), :], dot_)
                delta = delta + jnp.sum(p * dp, axis=0, keepdims=True)
                probs.append(p)
                grads.append(dp)
            dqt = jnp.zeros((size, BLOCK), jnp.float32)
            for j in range(i + 1):
                ds = probs[j] * (grads[j] - delta)
                if j == i:
                    diag_sum[...] += ds
                elif j == i - 1:
                    side_sum[...] += ds
                else:
                    far = far + jnp.sum(ds, axis=0, keepdims=True)
                low = ds.astype(jnp.bfloat16)
                dk_ref[:, block_of(j)] += dot_nt(qt, low)
                dv_ref[:, block_of(j)] += dot_nt(dot_, probs[j].astype(jnp.bfloat16))
                dqt = dqt + dot_nn(kt_ref[:, block_of(j)], low)
            dq_ref[:, block_of(i)] = (dqt * scale).astype(jnp.bfloat16)
        for c in range(parts):
            at = slice(c * rows, (c + 1) * rows)
            sent_ref[c, :size, :] = dq_ref[:, at]
            sent_ref[c, size : 2 * size, :] = dk_ref[:, at].astype(jnp.bfloat16)
            sent_ref[c, 2 * size :, :] = dv_ref[:, at].astype(jnp.bfloat16)
        bias_ref[0:1, :] = far

    start_all([back])

    @pl.when(is_head)
    def _():
        grad_ref[:size, :] = dq_ref[...]
        grad_ref[size : 2 * size, :] = dk_ref[...].astype(jnp.bfloat16)
        grad_ref[2 * size :, :] = dv_ref[...].astype(jnp.bfloat16)
        far = bias_ref[0:1, :] + jnp.sum(side_sum[:half, :], axis=0, keepdims=True)
        far_half = jnp.sum(side_sum[half:, half:], axis=0, keepdims=True)
        far = far + jnp.concatenate([jnp.zeros_like(far_half), far_half], axis=1)
        diag_bucket = near_buckets(buckets, 0, BLOCK, BLOCK)
        side_bucket = near_buckets(buckets, half, half, half)
        for b in range(buckets):
            one = jnp.sum(jnp.where(diag_bucket == b, diag_sum[...], 0.0), axis=0, keepdims=True)
            two = jnp.sum(
                jnp.where(side_bucket == b, side_sum[half:, :half], 0.0), axis=0, keepdims=True
            )
            row = one + jnp.concatenate([two, jnp.zeros_like(two)], axis=1)
            if b == buckets - 1:
                row = row + far
            bias_ref[b : b + 1, :] = row

    experts.wait()
    terms.wait()
    back.wait()
    for m in (arrive, back, experts, terms):
        m.wait_sent()


def attention_backward(sizes, do, expert_out, terms, qkv, stat, table, bounds):
    n_ctx, n_exp = sizes["ctx"], sizes["exp"]
    heads, size, rows = do.shape
    buckets = table.shape[0]
    seq = n_ctx * rows
    low, full = jnp.bfloat16, jnp.float32
    return pl.pallas_call(
        functools.partial(backward_kernel, sizes, heads, buckets),
        out_shape=[
            jax.ShapeDtypeStruct((heads, 3 * size, rows), low),
            jax.ShapeDtypeStruct(expert_out.shape, low),
            jax.ShapeDtypeStruct(terms.shape, low),
            jax.ShapeDtypeStruct((3 * size, seq), low),
            jax.ShapeDtypeStruct((buckets, BLOCK), full),
        ],
        in_specs=any_space(3) + in_vmem(2) + in_smem(2),
        out_specs=any_space(3) + in_vmem(2),
        scratch_shapes=[
            pltpu.VMEM((n_ctx, size, rows), low),
            pltpu.VMEM((n_ctx, 3 * size, rows), low),
            pltpu.VMEM((seq, size), low),
            pltpu.VMEM((seq, size), low),
            pltpu.VMEM((size, seq), low),
            pltpu.VMEM((size, seq), low),
            pltpu.VMEM((size, seq), full),
            pltpu.VMEM((size, seq), full),
            pltpu.VMEM((BLOCK, BLOCK), full),
            pltpu.VMEM((BLOCK // 2, BLOCK // 2), full),
            pltpu.VMEM((BLOCK, BLOCK), full),
            pltpu.VMEM((BLOCK, BLOCK), full),
        ]
        + move_sems(n_ctx)
        + move_sems(n_ctx)
        + move_sems(n_exp)
        + move_sems(n_exp),
        compiler_params=remote_params(3),
        cost_estimate=cost(20_000_000_000, 60_000_000, 2_400_000),
        name="attention_backward",
    )(do, expert_out, terms, qkv, stat, table, bounds)


def expert_kernel(
    rows_ref, g_ref, gate_ref, up_ref, down_ref, out_ref, back_ref, dgate_ref, wg_ref,
    dy_ref, sum_out, sum_back,
):
    step = pl.program_id(0)
    count, width = rows_ref.shape
    sources = gate_ref.shape[0]
    cap = count // sources

    @pl.when(step == 0)
    def _():
        lanes = jnp.concatenate([gate_ref[s, 0:1, :] for s in range(sources)], axis=0)
        columns = lanes.T
        for s in range(sources):
            at = slice(s * cap, (s + 1) * cap)
            gate = columns[:cap, s : s + 1]
            dy_ref[at, :] = (gate * g_ref[at, :].astype(jnp.float32)).astype(jnp.bfloat16)
        sum_out[...] = jnp.zeros_like(sum_out)
        sum_back[...] = jnp.zeros_like(sum_back)

    rows, dy = rows_ref[...], dy_ref[...]
    up, down = up_ref[0], down_ref[0]
    x = dot_nt(rows, up)
    c, a = math.sqrt(2.0 / math.pi), 0.044715
    square = x * x
    t = jnp.tanh(c * x * (1.0 + a * square))
    half = 0.5 * (1.0 + t)
    hidden = (x * half).astype(jnp.bfloat16)
    slope = half + 0.5 * x * (1.0 - t * t) * (c * (1.0 + 3.0 * a * square))
    dpre = (dot_nt(dy, down) * slope).astype(jnp.bfloat16)
    wg_ref[:, :width] = dot_tn(dpre, rows).astype(jnp.bfloat16)
    wg_ref[:, width:] = dot_tn(hidden, dy).astype(jnp.bfloat16)
    sum_out[...] += dot_nn(hidden, down)
    sum_back[...] += dot_nn(dpre, up)

    @pl.when(step == pl.num_programs(0) - 1)
    def _():
        back_ref[...] = sum_back[...].astype(jnp.bfloat16)
        out = sum_out[...].astype(jnp.bfloat16)
        out_ref[...] = out
        dgate = jnp.sum(out.astype(jnp.float32) * g_ref[...].astype(jnp.float32), axis=1, keepdims=True)
        lane = lax.broadcasted_iota(jnp.int32, (cap, 128), 1)
        columns = jnp.zeros((cap, 128), jnp.float32)
        for s in range(sources):
            columns = jnp.where(lane == s, dgate[s * cap : (s + 1) * cap, :], columns)
        turned = jnp.concatenate([columns] * (128 // cap), axis=0).T
        for s in range(sources):
            dgate_ref[s] = jnp.broadcast_to(turned[s : s + 1, :], (8, 128))


def run_expert(rows, g, gates, weights):
    count, width = rows.shape
    hidden = weights.shape[1]
    tile = 256
    low, full = jnp.bfloat16, jnp.float32
    whole = lambda shape: pl.BlockSpec(shape, lambda f: (0,) * len(shape))
    return pl.pallas_call(
        expert_kernel,
        grid=(hidden // tile,),
        out_shape=[
            jax.ShapeDtypeStruct((count, width), low),
            jax.ShapeDtypeStruct((count, width), low),
            jax.ShapeDtypeStruct(gates.shape, full),
            jax.ShapeDtypeStruct((hidden, 2 * width), low),
        ],
        in_specs=[
            whole((count, width)),
            whole((count, width)),
            whole(gates.shape),
            pl.BlockSpec((1, tile, width), lambda f: (0, f, 0)),
            pl.BlockSpec((1, tile, width), lambda f: (1, f, 0)),
        ],
        out_specs=[
            whole((count, width)),
            whole((count, width)),
            whole(gates.shape),
            pl.BlockSpec((tile, 2 * width), lambda f: (f, 0)),
        ],
        scratch_shapes=[
            pltpu.VMEM((count, width), low),
            pltpu.VMEM((count, width), full),
            pltpu.VMEM((count, width), full),
        ],
        compiler_params=pltpu.CompilerParams(vmem_limit_bytes=VMEM_BYTES),
        cost_estimate=cost(14_500_000_000, 24_000_000, 1_600_000),
        name="run_expert",
    )(rows, g, gates, weights, weights)


def total_kernel(
    sizes, heads, takers, head_in, small_in, out_in, qkv_out, weight_out, small_out, table_out,
    head_parts, small_parts, out_parts, head_sent, small_sent, out_sent,
    head_all, small_all, out_all, *sems,
):
    share, three = head_in.shape[1:]
    size = three // 3
    half = share // 2
    width = heads * size
    sixteen = out_sent.shape[0]
    me = lax.axis_index("ctx")
    greet(sizes, ["ctx", "exp"])
    first = [
        Move(sizes, "exp", head_in, head_parts, sems[0:3], split=True),
        Move(sizes, "exp", small_in, small_parts, sems[3:6], split=True),
        Move(sizes, "ctx", out_in, out_parts, sems[6:9], split=True, takers=takers),
    ]
    second = [
        Move(sizes, "ctx", head_sent, head_all, sems[9:12], senders=heads),
        Move(sizes, "ctx", small_sent, small_all, sems[12:15]),
        Move(sizes, "ctx", out_sent, out_all, sems[15:18], senders=takers),
    ]
    start_all(first)
    first[0].wait()
    total = head_parts[0].astype(jnp.float32)
    for s in range(1, sizes["exp"]):
        total = total + head_parts[s].astype(jnp.float32)
    total = total.astype(jnp.bfloat16)
    head_sent[:share, :] = total[:, : 2 * size]
    head_sent[share:, :] = jnp.concatenate(
        [total[:half, 2 * size :], total[half:, 2 * size :]], axis=1
    )
    start_all(second[:1])
    first[1].wait()
    little = small_parts[0]
    for s in range(1, sizes["exp"]):
        little = little + small_parts[s]
    small_sent[...] = little
    start_all(second[1:2])
    first[2].wait()

    @pl.when(me < takers)
    def _():
        weight = out_parts[0].astype(jnp.float32)
        for s in range(1, sizes["ctx"]):
            weight = weight + out_parts[s].astype(jnp.float32)
        out_sent[...] = weight.astype(jnp.bfloat16)

    start_all(second[2:])
    second[0].wait()
    for h in range(heads):
        got = head_all[h].astype(jnp.float32)
        at = h * size
        qkv_out[:, at : at + size] = got[:share, :size]
        qkv_out[:, width + at : width + at + size] = got[:share, size:]
        qkv_out[:half, 2 * width + at : 2 * width + at + size] = got[share:, :size]
        qkv_out[half:, 2 * width + at : 2 * width + at + size] = got[share:, size:]
    second[1].wait()
    sums = small_all[0]
    for s in range(1, sizes["ctx"]):
        sums = sums + small_all[s]
    small_out[...] = sums
    for h in range(heads):
        table_out[h : h + 1, :] = small_all[h, 0:1, :]
    second[2].wait()
    for s in range(takers):
        weight_out[s * sixteen : (s + 1) * sixteen, :] = out_all[s].astype(jnp.float32)
    for m in first + second:
        m.wait_sent()


def total_dense(sizes, heads, head_terms, small, out_terms):
    n_ctx, n_exp = sizes["ctx"], sizes["exp"]
    _, share, three = head_terms.shape
    takers, sixteen, width = out_terms.shape
    low, full = jnp.bfloat16, jnp.float32
    return pl.pallas_call(
        functools.partial(total_kernel, sizes, heads, takers),
        out_shape=[
            jax.ShapeDtypeStruct((share, 3 * width), full),
            jax.ShapeDtypeStruct((share, width), full),
            jax.ShapeDtypeStruct(small.shape[1:], full),
            jax.ShapeDtypeStruct((heads, 128), full),
        ],
        in_specs=in_vmem(3),
        out_specs=in_vmem(4),
        scratch_shapes=[
            pltpu.VMEM(head_terms.shape, low),
            pltpu.VMEM(small.shape, full),
            pltpu.VMEM((n_ctx, sixteen, width), low),
            pltpu.VMEM((share * 3 // 2, 128), low),
            pltpu.VMEM(small.shape[1:], full),
            pltpu.VMEM((sixteen, width), low),
            pltpu.VMEM((heads, share * 3 // 2, 128), low),
            pltpu.VMEM((n_ctx,) + small.shape[1:], full),
            pltpu.VMEM((takers, sixteen, width), low),
        ]
        + move_sems(n_exp)
        + move_sems(n_exp)
        + move_sems(n_ctx)
        + move_sems(n_ctx)
        + move_sems(n_ctx)
        + move_sems(n_ctx),
        compiler_params=remote_params(4),
        cost_estimate=cost(0, 60_000_000),
        name="total_dense",
    )(head_terms, small, out_terms)


def split_kernel(both_ref, up_ref, down_ref):
    width = up_ref.shape[1]
    up_ref[...] = both_ref[:, :width].astype(jnp.float32)
    down_ref[...] = both_ref[:, width:].astype(jnp.float32)


def split_weights(both):
    rows, width = both.shape[0], both.shape[1] // 2
    return pl.pallas_call(
        split_kernel,
        out_shape=[jax.ShapeDtypeStruct((rows, width), jnp.float32)] * 2,
        in_specs=in_vmem(1),
        out_specs=in_vmem(2),
        compiler_params=pltpu.CompilerParams(vmem_limit_bytes=8 * 1024 * 1024),
        cost_estimate=cost(0, 2_000_000),
        name="split_weights",
    )(both)


def rms_scale(values, gain_row):
    return (
        values * lax.rsqrt(jnp.mean(values * values, axis=-1, keepdims=True) + epsilon) * gain_row
    )


def local(
    sizes,
    block_in,
    attn_gain,
    moe_gain,
    query_key_value_weight,
    output_matrix,
    routing_weight,
    bias_table,
    up_weight,
    down_weight,
    routes,
    doc_lengths,
    cotangent,
):
    low, full = jnp.bfloat16, jnp.float32
    n_ctx, n_exp = sizes["ctx"], sizes["exp"]
    rows, width = block_in.shape[1:]
    seq_len = rows * n_ctx
    share = width // n_exp
    own_buckets, heads = bias_table.shape
    buckets = own_buckets * n_exp
    size = width // heads
    experts = routing_weight.shape[1]
    x_in = block_in[0].astype(full)
    g_low = cotangent[0]
    grad_out = g_low.astype(full)

    expert_weights = lax.all_gather(
        jnp.concatenate([up_weight, down_weight], axis=0), "ctx", axis=1, tiled=True
    )

    lanes = lambda a: jnp.pad(a, ((0, 0), (0, 128 - a.shape[1])))
    small = jnp.concatenate(
        [lanes(attn_gain[None]), lanes(moe_gain[None]), lanes(bias_table), lanes(routing_weight.T)],
        axis=0,
    )
    small = jnp.pad(small, ((0, -small.shape[0] % 16), (0, 0)))
    qkv_full, dense = gather_dense(sizes, query_key_value_weight, small)
    qkv_full = qkv_full.reshape(width, 3 * width)
    gain_one = dense[:, 0, :share].reshape(width).astype(full)
    gain_two = dense[:, 1, :share].reshape(width).astype(full)
    table_full = dense[:, 2 : 2 + own_buckets, :heads].reshape(buckets, heads).astype(full)
    router_t = dense[:, 2 + own_buckets : 2 + own_buckets + experts, :share]
    router_t = jnp.transpose(router_t, (1, 0, 2)).reshape(experts, width)
    head = jnp.minimum(lax.axis_index("ctx"), heads - 1)
    table_head = lax.dynamic_slice_in_dim(table_full, head, 1, 1)[:, 0]
    bounds = jnp.cumsum(doc_lengths[0]).astype(jnp.int32)

    route = routes[0]
    choose = (route[:, :, None] == jnp.arange(experts, dtype=jnp.int32)).astype(full)
    capacity = min(rows, 4 * rows // experts)
    flat_routes = route.reshape(2 * rows)
    marks = (flat_routes[:, None] == jnp.arange(experts, dtype=jnp.int32)).astype(full)
    before = jnp.asarray(np.tril(np.ones((2 * rows, 2 * rows), np.float32), -1), low)
    rank = jnp.sum(marks * jnp.dot(before, marks.astype(low), preferred_element_type=full), axis=-1)
    slot = (flat_routes * capacity + rank.astype(jnp.int32)).reshape(rows, 2)
    slots = jnp.arange(experts * capacity, dtype=jnp.int32)
    hit = [slots[:, None] == slot[:, c][None, :] for c in range(2)]
    either = (hit[0] | hit[1]).astype(low)
    found = [(slot[:, c][:, None] == slots[None, :]) for c in range(2)]
    piece = (experts, capacity, width)
    send_g = jnp.dot(either, g_low, preferred_element_type=full).astype(low)

    h_first = lax.optimization_barrier(rms_scale(x_in, gain_one).astype(low))
    h_all = lax.all_gather(h_first, "ctx", axis=0, tiled=True)
    qkv_t = lax.dot_general(
        qkv_full, h_first, (((0,), (1,)), ((), ())), preferred_element_type=full
    ).astype(low)
    qkv_t = jnp.transpose(qkv_t.reshape(3, heads, size, rows), (1, 0, 2, 3)).reshape(
        heads, 3 * size, rows
    )
    mixed, proj_full, g_rows, qkv_head, stat = attention_forward(
        sizes, qkv_t, output_matrix, send_g.reshape(piece), table_head, bounds
    )
    attended_t = mixed.reshape(width, rows)
    proj_full = proj_full.reshape(width, width)

    x_mid = x_in + dot_tn(attended_t, proj_full)
    h_second = rms_scale(x_mid, gain_two).astype(low)
    routing_logits = dot_nt(h_second, router_t)
    gates = jax.nn.softmax(jnp.sum(choose * routing_logits[:, None, :], axis=-1), axis=-1)
    send_rows = jnp.dot(either, h_second, preferred_element_type=full).astype(low)
    gate_slots = sum(
        jnp.sum(jnp.where(hit[c], gates[:, c][None, :], 0.0), axis=1) for c in range(2)
    )
    gate_slots = jnp.broadcast_to(
        lanes(gate_slots.reshape(experts, capacity))[:, None, :], (experts, 8, 128)
    )
    expert_rows, gate_rows = swap_experts(sizes, 5, send_rows.reshape(piece), gate_slots)
    expert_out, expert_back, dgate, weight_terms = run_expert(
        expert_rows.reshape(experts * capacity, width),
        g_rows.reshape(experts * capacity, width),
        gate_rows,
        expert_weights,
    )
    h_all, weight_terms = lax.optimization_barrier((h_all, weight_terms))
    weight_grads = lax.psum_scatter(weight_terms, "ctx", scatter_dimension=0, tiled=True)
    grad_back, dgate = swap_experts(sizes, 6, expert_back.reshape(piece), dgate)

    grad_back = grad_back.reshape(experts * capacity, width)
    dgate = dgate[:, 0, :capacity].reshape(1, experts * capacity)
    grad_gates = jnp.stack(
        [jnp.sum(jnp.where(found[c], dgate, 0.0), axis=1) for c in range(2)], axis=-1
    )
    grad_chosen = gates * (grad_gates - jnp.sum(gates * grad_gates, axis=-1, keepdims=True))
    grad_logits = jnp.sum(choose * grad_chosen[:, :, None], axis=1).astype(low)
    grad_h_second = jnp.dot(
        (found[0] | found[1]).astype(low), grad_back, preferred_element_type=full
    ) + jnp.dot(grad_logits, router_t, preferred_element_type=full)
    grad_x_norm, grad_gain_two = jax.vjp(rms_scale, x_mid, gain_two)[1](grad_h_second)
    grad_x_mid = grad_out + grad_x_norm
    grad_proj = grad_x_mid.astype(low)
    grad_attended = dot_nt(proj_full, grad_proj).astype(low).reshape(heads, size, rows)
    out_terms = jnp.dot(attended_t, grad_proj, preferred_element_type=full).astype(low)

    grad_qkv_t, returned, out_parts, grad_head, bias_rows = attention_backward(
        sizes,
        grad_attended,
        expert_out.reshape(piece),
        out_terms.reshape(n_exp, share, width),
        qkv_head,
        stat,
        table_head,
        bounds,
    )
    grad_qkv_t = jnp.transpose(
        grad_qkv_t.reshape(heads, 3, size, rows), (1, 0, 2, 3)
    ).reshape(3 * width, rows)
    grad_h_first = lax.dot_general(
        grad_qkv_t, qkv_full, (((0,), (1,)), ((), ())), preferred_element_type=full
    )
    grad_x_first, grad_gain_one = jax.vjp(rms_scale, x_in, gain_one)[1](grad_h_first)
    grad_in = (grad_x_mid + grad_x_first)[None]
    grad_router = dot_tn(grad_logits, h_second).reshape(experts, n_exp, share)
    head_terms = (
        lax.dot_general(h_all, grad_head, (((0,), (1,)), ((), ())), preferred_element_type=full)
        .astype(low)
        .reshape(n_exp, share, 3 * size)
    )
    bias_part = jnp.sum(bias_rows, axis=1).reshape(n_exp, own_buckets)
    first_row = jnp.concatenate([grad_gain_one.reshape(n_exp, share), bias_part], axis=1)
    totals = jnp.concatenate(
        [
            lanes(first_row)[:, None, :],
            lanes(grad_gain_two.reshape(n_exp, share))[:, None, :],
            jnp.pad(jnp.transpose(grad_router, (1, 0, 2)), ((0, 0), (0, 0), (0, 128 - share))),
        ],
        axis=1,
    )
    totals = jnp.pad(totals, ((0, 0), (0, -totals.shape[1] % 8), (0, 0)))
    out_sum = jnp.sum(out_parts.astype(full), axis=0).astype(low).reshape(share // 16, 16, width)
    grad_qkv, grad_out_weight, sums, table_rows = total_dense(
        sizes, heads, head_terms, totals, out_sum
    )
    returned = returned.reshape(experts * capacity, width)
    picked = jnp.dot(
        jnp.concatenate(found, axis=0).astype(low), returned, preferred_element_type=full
    )
    block_out = x_mid + (gates[:, :1] * picked[:rows] + gates[:, 1:] * picked[rows:])
    grad_up, grad_down = split_weights(weight_grads)
    return (
        block_out.astype(low)[None],
        grad_in,
        sums[0, :share],
        sums[1, :share],
        grad_qkv,
        grad_out_weight,
        sums[2 : 2 + experts, :share].T,
        table_rows[:, share : share + own_buckets].T,
        grad_up[None],
        grad_down[None],
    )


def solution(mesh):
    sizes = {name: mesh.shape[name] for name in ("ctx", "exp")}
    tokens = P("exp", "ctx", None)
    row_split = P("exp", None)
    return jax.shard_map(
        functools.partial(local, sizes),
        mesh=mesh,
        in_specs=(
            tokens,
            P("exp"),
            P("exp"),
            row_split,
            row_split,
            row_split,
            row_split,
            tokens,
            tokens,
            tokens,
            row_split,
            tokens,
        ),
        out_specs=(
            tokens,
            tokens,
            P("exp"),
            P("exp"),
            row_split,
            row_split,
            row_split,
            row_split,
            tokens,
            tokens,
        ),
        check_vma=False,
    )
```

profile of v0, /device:TPU:1, one launch (start us, length us, event | category | flops | bytes accessed | tf_op | source)
XLA Modules:
  0.0 282.2 jit_solution(13865041417157646098)
XLA Ops:
  7.2 1.9 pad_maximum_fusion
  11.0 28.3 %gather_dense.1 = (bf16[8,96,2304]{2,1,0:T(8,128)(2,1)S(1)}, bf16[8,16,128]{2,1,0:T(8,128)(2,1)S(1)}) custom-call(bf16[96,2304]{1,0:T(8,128)(2,1)S(1)} %copy-done.15, bf16[16,128]{1,0:T(8,128)(2,1)S(1)} %pad.43.s_ref), custom_call_target="tpu_custom_call" | custom-call | bytes 40000000 | tf_op jit(solution)/shard_map/gather_dense/pallas_call | solution.py:214
  41.1 1.7 fusion.7
  43.6 1.4 copy.53
  45.0 1.5 eq.85
  48.2 1.5 convert_element_type.115
  49.7 2.1 convolution_convert_fusion
  57.0 1.4 reshape.269
  58.4 1.5 copy.56
  64.3 35.6 %attention_forward.1 = (bf16[12,64,128]{2,1,0:T(8,128)(2,1)S(1)}, bf16[8,96,768]{2,1,0:T(8,128)(2,1)S(1)}, bf16[8,64,768]{2,1,0:T(8,128)(2,1)S(1)}, bf16[16,192,128]{2,1,0:T(8,128)(2,1)S(1)}, f32[8,256]{1,0:T(8,128)S(1)}) custom-call(bf16[12,192,128]{2,1,0:T(8,128)(2,1)S(1)} %bitcast.106, bf16[96,768]{1,0:T(8,128)(2,1)S(1)} %copy-done.22, ...), custom_call_target="tpu_custom_call" | custom-call | flops 12000000000 | bytes 50000000 | tf_op jit(solution)/shard_map/attention_forward/pallas_call | solution.py:411
  108.4 1.3 add.82
  111.8 14.7 %swap_experts_5.1 = (bf16[8,64,768]{2,1,0:T(8,128)(2,1)S(1)}, f32[8,8,128]{2,1,0:T(8,128)S(1)}) custom-call(bf16[8,64,768]{2,1,0:T(8,128)(2,1)S(1)} %bitcast.96, f32[8,8,128]{2,1,0:T(8,128)S(1)} %broadcast_in_dim.99.b_ref), custom_call_target="tpu_custom_call" | custom-call | bytes 30000000 | tf_op jit(solution)/shard_map/swap_experts_5/pallas_call | solution.py:239
  131.0 23.3 %run_expert.1 = (bf16[512,768]{1,0:T(8,128)(2,1)S(1)}, bf16[512,768]{1,0:T(8,128)(2,1)S(1)}, f32[8,8,128]{2,1,0:T(8,128)S(1)}, bf16[3072,1536]{1,0:T(8,128)(2,1)S(1)}) custom-call(bf16[512,768]{1,0:T(8,128)(2,1)S(1)} %bitcast.111, bf16[512,768]{1,0:T(8,128)(2,1)S(1)} %bitcast.113, f32[8,8,128]{2,1,0:T(8,128)S(1)} %copy-done.24, ...), custom_call_target="tpu_custom_call" | custom-call | flops 14499999744 | bytes 24000000 | tf_op jit(solution)/shard_map/run_expert/pallas_call | solution.py:665
  154.3 3.6 %copy-done = bf16[3072,1536]{1,0:T(8,128)(2,1)} copy-done((bf16[3072,1536]{1,0:T(8,128)(2,1)}, bf16[3072,1536]{1,0:T(8,128)(2,1)S(1)}, u32[]{:S(2)}) %copy-start) | copy-done | bytes 9437208
  160.4 1.5 iota_compare_fusion
  163.7 13.1 %swap_experts_6.1 = (bf16[8,64,768]{2,1,0:T(8,128)(2,1)S(1)}, f32[8,8,128]{2,1,0:T(8,128)S(1)}) custom-call(bf16[8,64,768]{2,1,0:T(8,128)(2,1)S(1)} %bitcast.101, f32[8,8,128]{2,1,0:T(8,128)S(1)} %copy-done.17), custom_call_target="tpu_custom_call" | custom-call | bytes 30000000 | tf_op jit(solution)/shard_map/swap_experts_6/pallas_call | solution.py:239
  178.3 1.3 broadcast_in_dim.100
  182.7 1.5 fusion.18
  184.2 2.1 multiply_reduce_fusion
  188.9 37.2 %attention_backward.1 = (bf16[12,192,128]{2,1,0:T(8,128)(2,1)S(1)}, bf16[8,64,768]{2,1,0:T(8,128)(2,1)S(1)}, bf16[8,96,768]{2,1,0:T(8,128)(2,1)S(1)}, bf16[192,2048]{1,0:T(8,128)(2,1)S(1)}, f32[32,256]{1,0:T(8,128)S(1)}) custom-call(bf16[12,64,128]{2,1,0:T(8,128)(2,1)S(1)} %bitcast.108, bf16[8,64,768]{2,1,0:T(8,128)(2,1)S(1)} %bitcast.112, ...), custom_call_target="tpu_custom_call" | custom-call | flops 20000000000 | bytes 60000000 | tf_op jit(solution)/shard_map/attention_backward/pallas_call | solution.py:574
  226.3 2.1 fusion.8
  230.8 3.0 %convolution_convert_fusion.4 = bf16[768,192]{0,1:T(8,128)(2,1)S(1)} fusion(bf16[192,2048]{1,0:T(8,128)(2,1)} %copy-done.5, bf16[2048,768]{1,0:T(8,128)(2,1)} %all-gather.5.cloned.1.call-done), kind=kOutput, calls=%fused_computation.4 | convolution fusion | flops 604127232 | bytes 4227072 | tf_op jit(solution)/shard_map/dot_general | solution.py:968
  234.3 32.7 %total_dense.1 = (f32[96,2304]{1,0:T(8,128)S(1)}, f32[96,768]{1,0:T(8,128)S(1)}, f32[16,128]{1,0:T(8,128)S(1)}, f32[12,128]{1,0:T(8,128)S(1)}) custom-call(bf16[8,96,192]{2,1,0:T(8,128)(2,1)S(1)} %bitcast.97, f32[8,16,128]{2,1,0:T(8,128)S(1)} %pad.48.small_in, bf16[6,16,768]{2,1,0:T(8,128)(2,1)S(1)} %bitcast.105), custom_call_target="tpu_custom_call" | custom-call | bytes 60000000 | tf_op jit(solution)/shard_map/total_dense/pallas_call | solution.py:774
  270.1 1.8 fusion.11
  (206 shorter events, 51.5 us)
Async XLA Ops:
  7.2 120.8 %all-gather.3.cloned.1.call-start = ((), (), s32[]{:S(2)}) async-start(), calls=%async_computation.1 | async-start | bytes 10027008 | tf_op jit(solution)/shard_map/all_gather | solution.py:860
  9.2 151.2 %all-gather.5.cloned.1.call-start = ((), (), s32[]{:S(2)}) async-start(), calls=%async_computation.2 | async-start | bytes 3342336 | tf_op jit(solution)/shard_map/all_gather | solution.py:897
  40.0 11.8 %copy-start.45 = (f32[768]{0:T(1024)}, f32[768]{0:T(1024)S(1)}, u32[]{:S(2)}) copy-start(f32[768]{0:T(1024)S(1)} %reshape.288) | copy-start | bytes 9220
  42.8 229.1 %reduce-scatter.2.cloned.1.call-start = ((), (), s32[]{:S(2)}) async-start(), calls=%async_computation.3 | async-start | bytes 10027008 | tf_op jit(solution)/shard_map/reduce_scatter | solution.py:929
  64.3 36.7 %copy-start.36 = (bf16[1,128,768]{2,1,0:T(8,128)(2,1)S(1)}, bf16[1,128,768]{2,1,0:T(8,128)(2,1)}, u32[]{:S(2)}) copy-start(bf16[1,128,768]{2,1,0:T(8,128)(2,1)} %param.13) | copy-start | bytes 589828
  64.3 38.2 %copy-start.44 = (f32[768]{0:T(1024)S(1)}, f32[768]{0:T(1024)}, u32[]{:S(2)}) copy-start(f32[768]{0:T(1024)} %reshape.290) | copy-start | bytes 9220
  179.7 7.2 %copy-start.32 = (f32[128,768]{1,0:T(8,128)S(1)}, f32[128,768]{1,0:T(8,128)}, u32[]{:S(2)}) copy-start(f32[128,768]{1,0:T(8,128)} %copy-done.31) | copy-start | bytes 1179652
  179.7 7.2 %copy-start.40 = (bf16[1,128,768]{2,1,0:T(8,128)(2,1)S(1)}, bf16[1,128,768]{2,1,0:T(8,128)(2,1)}, u32[]{:S(2)}) copy-start(bf16[1,128,768]{2,1,0:T(8,128)(2,1)} %param.24) | copy-start | bytes 589828
  179.7 8.2 %copy-start.7 = (bf16[12,64,128]{2,1,0:T(8,128)(2,1)S(1)}, bf16[12,64,128]{2,1,0:T(8,128)(2,1)}, u32[]{:S(2)}) copy-start(bf16[12,64,128]{2,1,0:T(8,128)(2,1)} %copy-done.6) | copy-start | bytes 589828
  184.2 4.2 %copy-start.2 = (bf16[8,96,768]{2,1,0:T(8,128)(2,1)S(1)}, bf16[8,96,768]{2,1,0:T(8,128)(2,1)}, u32[]{:S(2)}) copy-start(bf16[8,96,768]{2,1,0:T(8,128)(2,1)} %copy-done.1) | copy-start | bytes 3538948
  188.9 37.4 %copy-start.37 = (bf16[1,128,768]{2,1,0:T(8,128)(2,1)S(1)}, bf16[1,128,768]{2,1,0:T(8,128)(2,1)}, u32[]{:S(2)}) copy-start(bf16[1,128,768]{2,1,0:T(8,128)(2,1)} %param.13) | copy-start | bytes 589828
  188.9 37.4 %copy-start.46 = (f32[768]{0:T(1024)S(1)}, f32[768]{0:T(1024)}, u32[]{:S(2)}) copy-start(f32[768]{0:T(1024)} %copy-done.45) | copy-start | bytes 9220
  188.9 37.4 %copy-start.61 = (f32[128]{0:T(128)S(1)}, f32[128]{0:T(128)}, u32[]{:S(2)}) copy-start(f32[128]{0:T(128)} %copy-done.60) | copy-start | bytes 1540
  226.3 4.3 %copy-start.52 = (f32[768]{0:T(1024)S(1)}, f32[768]{0:T(1024)}, u32[]{:S(2)}) copy-start(f32[768]{0:T(1024)} %get-tuple-element.106) | copy-start | bytes 9220
  233.8 33.9 %copy-start.64 = (f32[128]{0:T(128)S(1)}, f32[128]{0:T(128)}, u32[]{:S(2)}) copy-start(f32[128]{0:T(128)} %copy-done.63) | copy-start | bytes 1540
  233.8 35.0 %copy-start.11 = (bf16[8,64,768]{2,1,0:T(8,128)(2,1)S(1)}, bf16[8,64,768]{2,1,0:T(8,128)(2,1)}, u32[]{:S(2)}) copy-start(bf16[8,64,768]{2,1,0:T(8,128)(2,1)} %copy-done.10) | copy-start | bytes 2359300
  233.8 35.0 %copy-start.41 = (pred[128,512]{1,0:T(32,128)(4,1)S(1)}, pred[128,512]{1,0:T(32,128)(4,1)}, u32[]{:S(2)}) copy-start(pred[128,512]{1,0:T(32,128)(4,1)} %get-tuple-element.126) | copy-start | bytes 196612
  233.9 35.0 %copy-start.42 = (pred[128,512]{1,0:T(32,128)(4,1)S(1)}, pred[128,512]{1,0:T(32,128)(4,1)}, u32[]{:S(2)}) copy-start(pred[128,512]{1,0:T(32,128)(4,1)} %get-tuple-element.127) | copy-start | bytes 196612
  233.9 35.4 %copy-start.33 = (f32[128,768]{1,0:T(8,128)S(1)}, f32[128,768]{1,0:T(8,128)}, u32[]{:S(2)}) copy-start(f32[128,768]{1,0:T(8,128)} %copy-done.31) | copy-start | bytes 1179652
  233.9 35.4 %copy-start.56 = (f32[128]{0:T(128)S(1)}, f32[128]{0:T(128)}, u32[]{:S(2)}) copy-start(f32[128]{0:T(128)} %copy-done.55) | copy-start | bytes 1540
  233.9 35.4 %copy-start.58 = (f32[128]{0:T(128)S(1)}, f32[128]{0:T(128)}, u32[]{:S(2)}) copy-start(f32[128]{0:T(128)} %copy-done.57) | copy-start | bytes 1540
  234.1 36.0 %copy-start.35 = (f32[128,768]{1,0:T(8,128)S(1)}, f32[128,768]{1,0:T(8,128)}, u32[]{:S(2)}) copy-start(f32[128,768]{1,0:T(8,128)} %copy-done.34) | copy-start | bytes 1179652
  234.1 36.0 %copy-start.47 = (f32[768]{0:T(1024)S(1)}, f32[768]{0:T(1024)}, u32[]{:S(2)}) copy-start(f32[768]{0:T(1024)} %copy-done.45) | copy-start | bytes 9220
  234.1 36.0 %copy-start.62 = (f32[128]{0:T(128)S(1)}, f32[128]{0:T(128)}, u32[]{:S(2)}) copy-start(f32[128]{0:T(128)} %copy-done.60) | copy-start | bytes 1540
  (45 other events, 69.3 us)
Sparse Core Ops, SparseCore 0:
  10.7 88.3 all-gather.2
  101.9 48.3 all-gather.4
  160.5 104.3 reduce-scatter.1
where the time goes:
time: 284 us; the launch traced here: 282 us
  Pallas kernels  186 us (65%)
  local copies, waits for them, and re-layouts  41.4 us (15%)
  other arithmetic  22.8 us (8%)
  matrix products  17.3 us (6%)
  between operations  14.6 us (5%)
    pallas_call x1, Pallas kernels, attention_backward(): pl.pallas_call(functools.partial(backward_kernel, sizes, heads, buckets),...  37.2 us
    pallas_call x1, Pallas kernels, attention_forward(): pl.pallas_call(functools.partial(forward_kernel, sizes, heads, buckets),...  35.6 us
    pallas_call x1, Pallas kernels, total_dense(): pl.pallas_call(functools.partial(total_kernel, sizes, heads, takers), out...  32.7 us
    pallas_call x1, Pallas kernels, gather_dense(): pl.pallas_call(kernel, out_shape=[jax.ShapeDtypeStruct((n,) + a.shape, a....  28.3 us
    pallas_call x2, Pallas kernels, swap_experts(): pl.pallas_call(kernel, out_shape=[jax.ShapeDtypeStruct(a.shape, a.dtype)...  27.8 us
    unnamed x137, local copies, waits for them, and re-layouts  25.9 us
    pallas_call x1, Pallas kernels, run_expert(): pl.pallas_call(expert_kernel, grid=(hidden // tile,), out_shape=[jax.Shap...  23.3 us
  transfers between devices with their start and end apart: 3, of which 0 were waited for; matrix products, arithmetic and copies ran while one was open for 20% of the time, Pallas kernels for 66%

commit v1 on v0

--- a/solution.py
+++ b/solution.py
@@ -197,32 +197,6 @@
     return pl.CostEstimate(flops=flops, bytes_accessed=moved, transcendentals=special)
 
 
-def gather_dense(sizes, weight, small):
-    n = sizes["exp"]
-
-    def kernel(w_ref, s_ref, w_out, s_out, *sems):
-        greet(sizes, ["exp"])
-        big = PairGather(sizes, w_ref, w_out, sems[:3])
-        little = Move(sizes, "exp", s_ref, s_out, sems[3:])
-        start_all([little])
-        big.start()
-        big.pass_on()
-        big.finish()
-        little.wait()
-        little.wait_sent()
-
-    return pl.pallas_call(
-        kernel,
-        out_shape=[jax.ShapeDtypeStruct((n,) + a.shape, a.dtype) for a in (weight, small)],
-        in_specs=any_space(2),
-        out_specs=any_space(2),
-        scratch_shapes=move_sems(n) + move_sems(n),
-        compiler_params=remote_params(1, 4 * 1024 * 1024),
-        cost_estimate=cost(0, 40_000_000),
-        name="gather_dense",
-    )(weight, small)
-
-
 def swap_experts(sizes, number, rows, values):
     n = sizes["exp"]
 
@@ -276,10 +250,10 @@
 
 def near_bias(table_ref, buckets, offset, rows, cols):
     bucket = near_buckets(buckets, offset, rows, cols)
-    last = table_ref[buckets - 1]
+    last = table_ref[buckets - 1 : buckets, 0:1]
     bias = jnp.zeros((rows, cols), jnp.float32)
     for b in range(buckets - 1):
-        bias = jnp.where(bucket == b, table_ref[b] - last, bias)
+        bias = jnp.where(bucket == b, table_ref[b : b + 1, 0:1] - last, bias)
     return bias
 
 
@@ -322,42 +296,127 @@
     return slice(j * BLOCK, (j + 1) * BLOCK)
 
 
-def forward_kernel(
+def bucket_values(small_ref, own_buckets, heads):
+    head = jnp.minimum(lax.axis_index("ctx"), heads - 1)
+    rows = jnp.concatenate(
+        [small_ref[e, 2 : 2 + own_buckets, :] for e in range(small_ref.shape[0])], axis=0
+    ).astype(jnp.float32)
+    lane = lax.broadcasted_iota(jnp.int32, rows.shape, 1)
+    value = jnp.sum(jnp.where(lane == head, rows, 0.0), axis=1, keepdims=True)
+    return jnp.broadcast_to(value, rows.shape)
+
+
+def full_row(small_ref, row, share):
+    pieces = [small_ref[e, row : row + 1, :share] for e in range(small_ref.shape[0])]
+    return jnp.concatenate(pieces, axis=1).astype(jnp.float32)
+
+
+def norm_rows(x, gain):
+    scale = lax.rsqrt(jnp.mean(x * x, axis=-1, keepdims=True) + epsilon)
+    return (x * scale * gain).astype(jnp.bfloat16)
+
+
+def columns_to_rows(column, groups):
+    cap = column.shape[0] // groups
+    lane = lax.broadcasted_iota(jnp.int32, (cap, 128), 1)
+    spread = jnp.zeros((cap, 128), jnp.float32)
+    for s in range(groups):
+        spread = jnp.where(lane == s, column[s * cap : (s + 1) * cap, :], spread)
+    return jnp.concatenate([spread] * (128 // cap), axis=0).T
+
+
+def front_kernel(
     sizes,
     heads,
-    buckets,
-    qkv_in,
+    experts,
+    own_buckets,
+    w_in,
+    small_in,
     proj_in,
-    g_in,
-    table_ref,
+    x_ref,
+    g_ref,
+    route_ref,
     bounds_ref,
-    mixed_out,
-    proj_out,
-    g_out,
+    w_ref,
+    small_ref,
+    proj_ref,
+    h_ref,
+    mid_ref,
+    second_ref,
+    info_ref,
+    mixed_ref,
     qkv_ref,
     stat_ref,
+    table_ref,
+    rows_out,
+    g_out,
+    gate_out,
+    qkv_sent,
     sent_ref,
     k_ref,
     vt_ref,
     diag_ref,
     side_ref,
+    rows_sent,
+    g_sent,
+    gate_sent,
     *sems,
 ):
-    parts, _, rows = qkv_ref.shape
-    size = sent_ref.shape[1]
+    n_exp = sizes["exp"]
+    parts, three, rows = qkv_ref.shape
+    size = three // 3
+    width = heads * size
+    share = width // n_exp
     blocks = parts * rows // BLOCK
     half = BLOCK // 2
-    greet(sizes, ["ctx", "exp"])
-    arrive = Move(sizes, "ctx", qkv_in, qkv_ref, sems[0:3], split=True, takers=heads)
-    back = Move(sizes, "ctx", sent_ref, mixed_out, sems[3:6], split=True, senders=heads)
-    proj = PairGather(sizes, proj_in, proj_out, sems[6:9])
-    grads = Move(sizes, "exp", g_in, g_out, sems[9:12], split=True)
-    start_all([arrive])
-    proj.start()
-    start_all([grads])
+    buckets = own_buckets * n_exp
+    cap = rows_sent.shape[1]
+    greet(sizes, ["exp", "ctx"])
+    weight = PairGather(sizes, w_in, w_ref, sems[0:3])
+    little = Move(sizes, "exp", small_in, small_ref, sems[3:6])
+    proj = PairGather(sizes, proj_in, proj_ref, sems[6:9])
+    grads = Move(sizes, "exp", g_sent, g_out, sems[9:12], split=True)
+    arrive = Move(sizes, "ctx", qkv_sent, qkv_ref, sems[12:15], split=True, takers=heads)
+    back = Move(sizes, "ctx", sent_ref, mixed_ref, sems[15:18], split=True, senders=heads)
+    hidden = Move(sizes, "exp", rows_sent, rows_out, sems[18:21], split=True)
+    gating = Move(sizes, "exp", gate_sent, gate_out, sems[21:24], split=True)
+    start_all([little])
+    weight.start()
+
+    expert = lax.broadcasted_iota(jnp.int32, (experts, rows), 0)
+    chosen = [(expert == route_ref[c : c + 1, :]).astype(jnp.float32) for c in range(2)]
+    earlier = lax.broadcasted_iota(jnp.int32, (rows, rows), 0) < lax.broadcasted_iota(
+        jnp.int32, (rows, rows), 1
+    )
+    count = dot_nn((chosen[0] + chosen[1]).astype(jnp.bfloat16), earlier.astype(jnp.bfloat16))
+    place = count + (expert * cap).astype(jnp.float32)
+    slot = [jnp.sum(chosen[c] * place, axis=0, keepdims=True) for c in range(2)]
+    slots = lax.broadcasted_iota(jnp.int32, (experts * cap, rows), 0).astype(jnp.float32)
+    hit = [slots == slot[c] for c in range(2)]
+    either = (hit[0] | hit[1]).astype(jnp.bfloat16)
+    send_g = dot_nn(either, g_ref[...]).astype(jnp.bfloat16)
+    for e in range(experts):
+        g_sent[e] = send_g[e * cap : (e + 1) * cap, :]
+
+    little.wait()
+    table_ref[...] = bucket_values(small_ref, own_buckets, heads)
+    x = x_ref[...].astype(jnp.float32)
+    h = norm_rows(x, full_row(small_ref, 0, share))
+    h_ref[...] = h
     diag_ref[...] = near_bias(table_ref, buckets, 0, BLOCK, BLOCK)
     side_ref[...] = near_bias(table_ref, buckets, half, half, half)
+    weight.pass_on()
+    proj.start()
+    weight.finish()
+    for at in range(0, 3 * width, 2 * rows):
+        piece = w_ref[:, :, at : at + 2 * rows].reshape(width, 2 * rows)
+        turned = dot_nn(h, piece).T.astype(jnp.bfloat16)
+        for begin in range(0, 2 * rows, size):
+            part, head = divmod((at + begin) // size, heads)
+            qkv_sent[head, part * size : (part + 1) * size, :] = turned[begin : begin + size, :]
+    start_all([arrive])
     proj.pass_on()
+    start_all([grads])
     arrive.wait()
 
     @pl.when(lax.axis_index("ctx") < heads)
@@ -394,46 +453,90 @@
 
     start_all([back])
     proj.finish()
+    back.wait()
+
+    attended = transposed(mixed_ref[...].reshape(width, rows))
+    mid = x + dot_nn(attended, proj_ref[...].reshape(width, width))
+    mid_ref[...] = mid
+    second = norm_rows(mid, full_row(small_ref, 1, share))
+    second_ref[...] = second
+    send = dot_nn(either, second).astype(jnp.bfloat16)
+    for e in range(experts):
+        rows_sent[e] = send[e * cap : (e + 1) * cap, :]
+    start_all([hidden])
+    begin = 2 + own_buckets
+    router = jnp.concatenate(
+        [small_ref[e, begin : begin + experts, :share] for e in range(n_exp)], axis=1
+    )
+    z = dot_nt(router, second)
+    picked = [jnp.sum(chosen[c] * z, axis=0, keepdims=True) for c in range(2)]
+    top = jnp.maximum(picked[0], picked[1])
+    raised = [jnp.exp(p - top) for p in picked]
+    gates = [r / (raised[0] + raised[1]) for r in raised]
+    column = sum(
+        jnp.sum(jnp.where(hit[c], gates[c], 0.0), axis=1, keepdims=True) for c in range(2)
+    )
+    turned = columns_to_rows(column, experts)
+    for e in range(experts):
+        gate_sent[e] = jnp.broadcast_to(turned[e : e + 1, :], (8, 128))
+    start_all([gating])
+    info_ref[...] = jnp.concatenate(
+        gates + slot + [route_ref[c : c + 1, :].astype(jnp.float32) for c in range(2)] + slot,
+        axis=0,
+    )
     grads.wait()
-    back.wait()
-    for m in (arrive, back, grads):
+    gating.wait()
+    hidden.wait()
+    for m in (little, grads, arrive, back, hidden, gating):
         m.wait_sent()
 
 
-def attention_forward(sizes, qkv, proj, g, table, bounds):
+def run_front(sizes, heads, experts, own_buckets, weight, small, proj, x, g, route_t, bounds):
     n_ctx, n_exp = sizes["ctx"], sizes["exp"]
-    heads, three, rows = qkv.shape
-    size = three // 3
-    buckets = table.shape[0]
+    rows, width = x.shape
+    size = width // heads
     seq = n_ctx * rows
+    cap = min(rows, 4 * rows // experts)
     low, full = jnp.bfloat16, jnp.float32
-    assert 2 * rows == BLOCK
+    assert 2 * rows == BLOCK and rows == 128 and 3 * width % (2 * rows) == 0
     return pl.pallas_call(
-        functools.partial(forward_kernel, sizes, heads, buckets),
+        functools.partial(front_kernel, sizes, heads, experts, own_buckets),
         out_shape=[
+            jax.ShapeDtypeStruct((n_exp,) + weight.shape, low),
+            jax.ShapeDtypeStruct((n_exp,) + small.shape, low),
+            jax.ShapeDtypeStruct((n_exp,) + proj.shape, low),
+            jax.ShapeDtypeStruct((rows, width), low),
+            jax.ShapeDtypeStruct((rows, width), full),
+            jax.ShapeDtypeStruct((rows, width), low),
+            jax.ShapeDtypeStruct((8, rows), full),
             jax.ShapeDtypeStruct((heads, size, rows), low),
-            jax.ShapeDtypeStruct((n_exp,) + proj.shape, low),
-            jax.ShapeDtypeStruct(g.shape, low),
-            jax.ShapeDtypeStruct((n_ctx, three, rows), low),
+            jax.ShapeDtypeStruct((n_ctx, 3 * size, rows), low),
             jax.ShapeDtypeStruct((seq // BLOCK, BLOCK), full),
+            jax.ShapeDtypeStruct((own_buckets * n_exp, 128), full),
+            jax.ShapeDtypeStruct((experts, cap, width), low),
+            jax.ShapeDtypeStruct((experts, cap, width), low),
+            jax.ShapeDtypeStruct((experts, 8, 128), full),
         ],
-        in_specs=any_space(3) + in_smem(2),
-        out_specs=any_space(3) + in_vmem(2),
+        in_specs=in_vmem(6) + in_smem(1),
+        out_specs=in_vmem(14),
         scratch_shapes=[
+            pltpu.VMEM((heads, 3 * size, rows), low),
             pltpu.VMEM((n_ctx, size, rows), low),
             pltpu.VMEM((seq, size), low),
             pltpu.VMEM((size, seq), low),
             pltpu.VMEM((BLOCK, BLOCK), full),
             pltpu.VMEM((BLOCK // 2, BLOCK // 2), full),
+            pltpu.VMEM((experts, cap, width), low),
+            pltpu.VMEM((experts, cap, width), low),
+            pltpu.VMEM((experts, 8, 128), full),
         ]
-        + move_sems(n_ctx)
-        + move_sems(n_ctx)
-        + move_sems(n_exp)
-        + move_sems(n_exp),
-        compiler_params=remote_params(2),
-        cost_estimate=cost(12_000_000_000, 50_000_000, 2_400_000),
-        name="attention_forward",
-    )(qkv, proj, g, table, bounds)
+        + move_sems(n_exp) * 4
+        + move_sems(n_ctx) * 2
+        + move_sems(n_exp) * 2,
+        compiler_params=remote_params(1),
+        cost_estimate=cost(60_000_000_000, 100_000_000, 2_400_000),
+        name="run_front",
+    )(weight, small, proj, x, g, route_t, bounds)
 
 
 def backward_kernel(
@@ -580,7 +683,7 @@
             jax.ShapeDtypeStruct((3 * size, seq), low),
             jax.ShapeDtypeStruct((buckets, BLOCK), full),
         ],
-        in_specs=any_space(3) + in_vmem(2) + in_smem(2),
+        in_specs=any_space(3) + in_vmem(3) + in_smem(1),
         out_specs=any_space(3) + in_vmem(2),
         scratch_shapes=[
             pltpu.VMEM((n_ctx, size, rows), low),
@@ -867,58 +970,49 @@
         axis=0,
     )
     small = jnp.pad(small, ((0, -small.shape[0] % 16), (0, 0)))
-    qkv_full, dense = gather_dense(sizes, query_key_value_weight, small)
+    capacity = min(rows, 4 * rows // experts)
+    piece = (experts, capacity, width)
+    bounds = jnp.cumsum(doc_lengths[0]).astype(jnp.int32)
+    (
+        qkv_full,
+        dense,
+        proj_full,
+        h_first,
+        x_mid,
+        h_second,
+        info,
+        mixed,
+        qkv_head,
+        stat,
+        table_head,
+        expert_rows,
+        g_rows,
+        gate_rows,
+    ) = run_front(
+        sizes,
+        heads,
+        experts,
+        own_buckets,
+        query_key_value_weight,
+        small,
+        output_matrix,
+        block_in[0],
+        g_low,
+        routes[0].T,
+        bounds,
+    )
+    h_all = lax.all_gather(h_first, "ctx", axis=0, tiled=True)
     qkv_full = qkv_full.reshape(width, 3 * width)
+    proj_full = proj_full.reshape(width, width)
+    attended_t = mixed.reshape(width, rows)
     gain_one = dense[:, 0, :share].reshape(width).astype(full)
     gain_two = dense[:, 1, :share].reshape(width).astype(full)
-    table_full = dense[:, 2 : 2 + own_buckets, :heads].reshape(buckets, heads).astype(full)
     router_t = dense[:, 2 + own_buckets : 2 + own_buckets + experts, :share]
     router_t = jnp.transpose(router_t, (1, 0, 2)).reshape(experts, width)
-    head = jnp.minimum(lax.axis_index("ctx"), heads - 1)
-    table_head = lax.dynamic_slice_in_dim(table_full, head, 1, 1)[:, 0]
-    bounds = jnp.cumsum(doc_lengths[0]).astype(jnp.int32)
-
-    route = routes[0]
-    choose = (route[:, :, None] == jnp.arange(experts, dtype=jnp.int32)).astype(full)
-    capacity = min(rows, 4 * rows // experts)
-    flat_routes = route.reshape(2 * rows)
-    marks = (flat_routes[:, None] == jnp.arange(experts, dtype=jnp.int32)).astype(full)
-    before = jnp.asarray(np.tril(np.ones((2 * rows, 2 * rows), np.float32), -1), low)
-    rank = jnp.sum(marks * jnp.dot(before, marks.astype(low), preferred_element_type=full), axis=-1)
-    slot = (flat_routes * capacity + rank.astype(jnp.int32)).reshape(rows, 2)
-    slots = jnp.arange(experts * capacity, dtype=jnp.int32)
-    hit = [slots[:, None] == slot[:, c][None, :] for c in range(2)]
-    either = (hit[0] | hit[1]).astype(low)
-    found = [(slot[:, c][:, None] == slots[None, :]) for c in range(2)]
-    piece = (experts, capacity, width)
-    send_g = jnp.dot(either, g_low, preferred_element_type=full).astype(low)
-
-    h_first = lax.optimization_barrier(rms_scale(x_in, gain_one).astype(low))
-    h_all = lax.all_gather(h_first, "ctx", axis=0, tiled=True)
-    qkv_t = lax.dot_general(
-        qkv_full, h_first, (((0,), (1,)), ((), ())), preferred_element_type=full
-    ).astype(low)
-    qkv_t = jnp.transpose(qkv_t.reshape(3, heads, size, rows), (1, 0, 2, 3)).reshape(
-        heads, 3 * size, rows
-    )
-    mixed, proj_full, g_rows, qkv_head, stat = attention_forward(
-        sizes, qkv_t, output_matrix, send_g.reshape(piece), table_head, bounds
-    )
-    attended_t = mixed.reshape(width, rows)
-    proj_full = proj_full.reshape(width, width)
-
-    x_mid = x_in + dot_tn(attended_t, proj_full)
-    h_second = rms_scale(x_mid, gain_two).astype(low)
-    routing_logits = dot_nt(h_second, router_t)
-    gates = jax.nn.softmax(jnp.sum(choose * routing_logits[:, None, :], axis=-1), axis=-1)
-    send_rows = jnp.dot(either, h_second, preferred_element_type=full).astype(low)
-    gate_slots = sum(
-        jnp.sum(jnp.where(hit[c], gates[:, c][None, :], 0.0), axis=1) for c in range(2)
-    )
-    gate_slots = jnp.broadcast_to(
-        lanes(gate_slots.reshape(experts, capacity))[:, None, :], (experts, 8, 128)
-    )
-    expert_rows, gate_rows = swap_experts(sizes, 5, send_rows.reshape(piece), gate_slots)
+    gates = info[:2].T
+    slots = jnp.arange(experts * capacity, dtype=jnp.int32).astype(full)
+    found = [info[2 + c][:, None] == slots[None, :] for c in range(2)]
+    choose = (routes[0][:, :, None] == jnp.arange(experts, dtype=jnp.int32)).astype(full)
     expert_out, expert_back, dgate, weight_terms = run_expert(
         expert_rows.reshape(experts * capacity, width),
         g_rows.reshape(experts * capacity, width),

time: 284 us -> 274 us (0.965)
  waiting for transfers between devices: 0.05 us -> 19.4 us
  local copies, waits for them, and re-layouts: 41.4 us -> 30.7 us
  other arithmetic: 22.8 us -> 12.5 us
  matrix products: 17.3 us -> 12 us
    all_gather x1, waiting for transfers between devices: 0.01 us -> 17.1 us  [local(): h_all = lax.all_gather(h_first, 'ctx', axis=0, tiled=True)]
    pallas_call x2 -> x1, Pallas kernels: 27.8 us -> 14.5 us  [swap_experts(): pl.pallas_call(kernel, out_shape=[jax.ShapeDtypeStruct(a.shape, a.dtype)...]
    pallas_call x2 -> x1, Pallas kernels: 63.9 us -> 74.5 us  [run_front(): pl.pallas_call(functools.partial(front_kernel, sizes, heads, experts, own...]
    dot_general x4 -> x0, matrix products: 5.75 us -> none  [the longest x1 2.06 us: local(): lax.dot_general(qkv_full, h_first, (((0,), (1,)), ((), ())), preferred_el...]
    convert_element_type x5 -> x2, other arithmetic: 3.09 us -> 0.03 us  [the longest x1 0.03 us: local(): gain_one = dense[:, 0, :share].reshape(width).astype(full)]
    unnamed x137 -> x99, local copies, waits for them, and re-layouts: 25.9 us -> 23.2 us
  transfers between devices with their start and end apart: 3 -> 3, of which waited for: 0 -> 2; matrix products, arithmetic and copies ran while one was open for 20% -> 11% of each run, Pallas kernels for 66% -> 67%
where the time goes in v1:
time: 274 us; the launch traced here: 273 us
  Pallas kernels  184 us (67%)
  local copies, waits for them, and re-layouts  30.7 us (11%)
  waiting for transfers between devices  19.4 us (7%)
  between operations  14.2 us (5%)
  other arithmetic  12.5 us (5%)
  matrix products  12 us (4%)
    pallas_call x1, Pallas kernels, run_front(): pl.pallas_call(functools.partial(front_kernel, sizes, heads, experts, own...  74.5 us
    pallas_call x1, Pallas kernels, attention_backward(): pl.pallas_call(functools.partial(backward_kernel, sizes, heads, buckets),...  36.4 us
    pallas_call x1, Pallas kernels, total_dense(): pl.pallas_call(functools.partial(total_kernel, sizes, heads, takers), out...  33.8 us
    pallas_call x1, Pallas kernels, run_expert(): pl.pallas_call(expert_kernel, grid=(hidden // tile,), out_shape=[jax.Shap...  23.3 us
    unnamed x99, local copies, waits for them, and re-layouts  23.2 us
    all_gather x1, waiting for transfers between devices, local(): h_all = lax.all_gather(h_first, 'ctx', axis=0, tiled=True)  17.1 us
    pallas_call x1, Pallas kernels, swap_experts(): pl.pallas_call(kernel, out_shape=[jax.ShapeDtypeStruct(a.shape, a.dtype)...  14.5 us
  transfers between devices with their start and end apart: 3, of which 2 were waited for; matrix products, arithmetic and copies ran while one was open for 11% of the time, Pallas kernels for 67%

profile of v1, /device:TPU:1, one launch (start us, length us, event | category | flops | bytes accessed | tf_op | source)
XLA Modules:
  0.0 272.7 jit_solution(327966154290727052)
XLA Ops:
  7.2 1.9 pad_maximum_fusion
  13.3 1.0 copy-done.16
  15.2 74.5 %run_front.1 = (bf16[8,96,2304]{2,1,0:T(8,128)(2,1)S(1)}, bf16[8,16,128]{2,1,0:T(8,128)(2,1)S(1)}, bf16[8,96,768]{2,1,0:T(8,128)(2,1)S(1)}, bf16[128,768]{1,0:T(...) custom-call(bf16[96,2304]{1,0:T(8,128)(2,1)S(1)} %copy-done.16, ...), custom_call_target="tpu_custom_call" | custom-call | flops 60000002048 | bytes 100000000 | tf_op jit(solution)/shard_map/run_front/pallas_call | solution.py:502
  89.8 1.8 copy-done.1
  97.1 2.2 all-gather.3.cloned.1.call-done.up_ref.down_ref
  99.3 1.1 copy-done.21
  100.4 1.1 copy-done.23
  101.5 23.3 %run_expert.1 = (bf16[512,768]{1,0:T(8,128)(2,1)S(1)}, bf16[512,768]{1,0:T(8,128)(2,1)S(1)}, f32[8,8,128]{2,1,0:T(8,128)S(1)}, bf16[3072,1536]{1,0:T(8,128)(2,1)S(1)}) custom-call(bf16[512,768]{1,0:T(8,128)(2,1)S(1)} %bitcast.97, bf16[512,768]{1,0:T(8,128)(2,1)S(1)} %bitcast.98, f32[8,8,128]{2,1,0:T(8,128)S(1)} %get-tuple-element.48.gate_ref, ...), custom_call_target="tpu_custom_call" | custom-call | flops 14499999744 | bytes 24000000 | tf_op jit(solution)/shard_map/run_expert/pallas_call | solution.py:768
  124.8 3.7 %copy-done = bf16[3072,1536]{1,0:T(8,128)(2,1)} copy-done((bf16[3072,1536]{1,0:T(8,128)(2,1)}, bf16[3072,1536]{1,0:T(8,128)(2,1)S(1)}, u32[]{:S(2)}) %copy-start) | copy-done | bytes 9437208
  130.0 17.1 %all-gather.5.cloned.1.call-done = bf16[2048,768]{1,0:T(8,128)(2,1)} async-done(((bf16[128,768]{1,0:T(8,128)(2,1)}), bf16[2048,768]{1,0:T(8,128)(2,1)}) %all-gather.5.cloned.1.call-update) | async-done | bytes 3145744 | tf_op jit(solution)/shard_map/all_gather | solution.py:1004
  152.2 14.5 %swap_experts_6.1 = (bf16[8,64,768]{2,1,0:T(8,128)(2,1)S(1)}, f32[8,8,128]{2,1,0:T(8,128)S(1)}) custom-call(bf16[8,64,768]{2,1,0:T(8,128)(2,1)S(1)} %bitcast.86, f32[8,8,128]{2,1,0:T(8,128)S(1)} %copy-done.12), custom_call_target="tpu_custom_call" | custom-call | bytes 30000000 | tf_op jit(solution)/shard_map/swap_experts_6/pallas_call | solution.py:213
  167.8 1.0 fusion.14
  168.8 1.8 multiply_reduce_fusion
  172.1 1.5 convolution_convert_fusion
  174.2 36.4 %attention_backward.1 = (bf16[12,192,128]{2,1,0:T(8,128)(2,1)S(1)}, bf16[8,64,768]{2,1,0:T(8,128)(2,1)S(1)}, bf16[8,96,768]{2,1,0:T(8,128)(2,1)S(1)}, bf16[192,2048]{1,0:T(8,128)(2,1)S(1)}, f32[32,256]{1,0:T(8,128)S(1)}) custom-call(bf16[12,64,128]{2,1,0:T(8,128)(2,1)S(1)} %bitcast.93, bf16[8,64,768]{2,1,0:T(8,128)(2,1)S(1)} %bitcast.96, ...), custom_call_target="tpu_custom_call" | custom-call | flops 20000000000 | bytes 60000000 | tf_op jit(solution)/shard_map/attention_backward/pallas_call | solution.py:677
  210.8 2.7 fusion.10
  214.2 1.4 reduce_sum.136
  215.6 1.3 reshape.189
  219.5 3.4 %convolution_convert_fusion.1 = bf16[768,192]{0,1:T(8,128)(2,1)} fusion(bf16[192,2048]{1,0:T(8,128)(2,1)S(1)} %get-tuple-element.65, bf16[2048,768]{1,0:T(8,128)(2,1)} %all-gather.5.cloned.1.call-done), kind=kOutput, calls=%fused_computation.1 | convolution fusion | flops 604127232 | bytes 4227072 | tf_op jit(solution)/shard_map/dot_general | solution.py:1062
  222.9 1.1 copy.35
  224.2 33.8 %total_dense.1 = (f32[96,2304]{1,0:T(8,128)S(1)}, f32[96,768]{1,0:T(8,128)S(1)}, f32[16,128]{1,0:T(8,128)S(1)}, f32[12,128]{1,0:T(8,128)S(1)}) custom-call(bf16[8,96,192]{2,1,0:T(8,128)(2,1)S(1)} %bitcast.83, f32[8,16,128]{2,1,0:T(8,128)S(1)} %pad.43.small_in, bf16[6,16,768]{2,1,0:T(8,128)(2,1)S(1)} %bitcast.89), custom_call_target="tpu_custom_call" | custom-call | bytes 60000000 | tf_op jit(solution)/shard_map/total_dense/pallas_call | solution.py:877
  260.3 2.1 fusion.6
  262.5 1.1 copy-done.5
  263.5 1.0 split_weights.1
  (143 shorter events, 27.4 us)
Async XLA Ops:
  7.2 92.1 %all-gather.3.cloned.1.call-start = ((), (), s32[]{:S(2)}) async-start(), calls=%async_computation.1 | async-start | bytes 10027008 | tf_op jit(solution)/shard_map/all_gather | solution.py:963
  9.2 138.0 %all-gather.5.cloned.1.call-start = ((), (), s32[]{:S(2)}) async-start(), calls=%async_computation.2 | async-start | bytes 3342336 | tf_op jit(solution)/shard_map/all_gather | solution.py:1004
  96.9 165.6 %reduce-scatter.2.cloned.1.call-start = ((), (), s32[]{:S(2)}) async-start(), calls=%async_computation.3 | async-start | bytes 10027008 | tf_op jit(solution)/shard_map/reduce_scatter | solution.py:1023
  124.8 3.7 %copy-start = (bf16[3072,1536]{1,0:T(8,128)(2,1)}, bf16[3072,1536]{1,0:T(8,128)(2,1)S(1)}, u32[]{:S(2)}) copy-start(bf16[3072,1536]{1,0:T(8,128)(2,1)S(1)} %get-tuple-element.73) | copy-start | bytes 28311556
  147.1 20.6 %copy-start.15 = (s32[1,128,2]{1,2,0:T(2,128)S(1)}, s32[1,128,2]{1,2,0:T(2,128)}, u32[]{:S(2)}) copy-start(s32[1,128,2]{1,2,0:T(2,128)} %param.21) | copy-start | bytes 3076
  147.2 24.1 %copy-start.7 = (bf16[1,128,768]{2,1,0:T(8,128)(2,1)S(1)}, bf16[1,128,768]{2,1,0:T(8,128)(2,1)}, u32[]{:S(2)}) copy-start(bf16[1,128,768]{2,1,0:T(8,128)(2,1)} %param.23) | copy-start | bytes 589828
  167.8 6.4 %copy-start.35 = (bf16[128,8]{0,1:T(8,128)(2,1)}, bf16[128,8]{0,1:T(8,128)(2,1)S(1)}, u32[]{:S(2)}) copy-start(bf16[128,8]{0,1:T(8,128)(2,1)S(1)} %select_reduce_fusion.2) | copy-start | bytes 6148
  168.8 5.4 %copy-start.19 = (bf16[512,768]{1,0:T(8,128)(2,1)S(1)}, bf16[512,768]{1,0:T(8,128)(2,1)}, u32[]{:S(2)}) copy-start(bf16[512,768]{1,0:T(8,128)(2,1)} %copy-done.18) | copy-start | bytes 2359300
  168.8 5.4 %copy-start.25 = (bf16[16,192,128]{2,1,0:T(8,128)(2,1)S(1)}, bf16[16,192,128]{2,1,0:T(8,128)(2,1)}, u32[]{:S(2)}) copy-start(bf16[16,192,128]{2,1,0:T(8,128)(2,1)} %copy-done.24) | copy-start | bytes 2359300
  168.8 5.4 %copy-start.27 = (f32[32,128]{1,0:T(8,128)S(1)}, f32[32,128]{1,0:T(8,128)}, u32[]{:S(2)}) copy-start(f32[32,128]{1,0:T(8,128)} %copy-done.26) | copy-start | bytes 49156
  168.8 5.4 %copy-start.29 = (f32[8,256]{1,0:T(8,128)S(1)}, f32[8,256]{1,0:T(8,128)}, u32[]{:S(2)}) copy-start(f32[8,256]{1,0:T(8,128)} %copy-done.28) | copy-start | bytes 24580
  174.2 36.5 %copy-start.2 = (bf16[8,96,2304]{2,1,0:T(8,128)(2,1)S(1)}, bf16[8,96,2304]{2,1,0:T(8,128)(2,1)}, u32[]{:S(2)}) copy-start(bf16[8,96,2304]{2,1,0:T(8,128)(2,1)} %copy-done.1) | copy-start | bytes 10616836
  174.2 36.5 %copy-start.33 = (f32[768]{0:T(1024)S(1)}, f32[768]{0:T(1024)}, u32[]{:S(2)}) copy-start(f32[768]{0:T(1024)} %reshape.194) | copy-start | bytes 9220
  174.2 36.5 %copy-start.42 = (f32[128]{0:T(128)S(1)}, f32[128]{0:T(128)}, u32[]{:S(2)}) copy-start(f32[128]{0:T(128)} %fusion.37) | copy-start | bytes 1540
  210.7 6.2 %copy-start.10 = (bf16[128,768]{1,0:T(8,128)(2,1)S(1)}, bf16[128,768]{1,0:T(8,128)(2,1)}, u32[]{:S(2)}) copy-start(bf16[128,768]{1,0:T(8,128)(2,1)} %copy-done.9) | copy-start | bytes 589828
  210.7 6.2 %copy-start.36 = (bf16[128,8]{0,1:T(8,128)(2,1)S(1)}, bf16[128,8]{0,1:T(8,128)(2,1)}, u32[]{:S(2)}) copy-start(bf16[128,8]{0,1:T(8,128)(2,1)} %copy-done.35) | copy-start | bytes 6148
  210.7 7.8 %copy-start.37 = (f32[768]{0:T(1024)S(1)}, f32[768]{0:T(1024)}, u32[]{:S(2)}) copy-start(f32[768]{0:T(1024)} %get-tuple-element.106) | copy-start | bytes 9220
  219.4 39.4 %copy-start.45 = (f32[128]{0:T(128)S(1)}, f32[128]{0:T(128)}, u32[]{:S(2)}) copy-start(f32[128]{0:T(128)} %copy-done.44) | copy-start | bytes 1540
  219.4 39.4 %copy-start.47 = (f32[128]{0:T(128)S(1)}, f32[128]{0:T(128)}, u32[]{:S(2)}) copy-start(f32[128]{0:T(128)} %get-tuple-element.109) | copy-start | bytes 1540
  219.4 40.5 %copy-start.31 = (pred[128,512]{1,0:T(32,128)(4,1)S(1)}, pred[128,512]{1,0:T(32,128)(4,1)}, u32[]{:S(2)}) copy-start(pred[128,512]{1,0:T(32,128)(4,1)} %get-tuple-element.118) | copy-start | bytes 196612
  219.4 40.5 %copy-start.32 = (pred[128,512]{1,0:T(32,128)(4,1)S(1)}, pred[128,512]{1,0:T(32,128)(4,1)}, u32[]{:S(2)}) copy-start(pred[128,512]{1,0:T(32,128)(4,1)} %get-tuple-element.119) | copy-start | bytes 196612
  222.9 37.4 %copy-start.40 = (f32[128]{0:T(128)S(1)}, f32[128]{0:T(128)}, u32[]{:S(2)}) copy-start(f32[128]{0:T(128)} %get-tuple-element.120) | copy-start | bytes 1540
  222.9 37.4 %copy-start.41 = (f32[128]{0:T(128)S(1)}, f32[128]{0:T(128)}, u32[]{:S(2)}) copy-start(f32[128]{0:T(128)} %get-tuple-element.121) | copy-start | bytes 1540
  222.9 37.4 %copy-start.43 = (f32[128]{0:T(128)S(1)}, f32[128]{0:T(128)}, u32[]{:S(2)}) copy-start(f32[128]{0:T(128)} %fusion.37) | copy-start | bytes 1540
  (27 other events, 30.1 us)
Sparse Core Ops, SparseCore 0:
  10.7 88.4 all-gather.2
  101.4 45.7 all-gather.4
  150.6 105.2 reduce-scatter.1

commit v2 on v1

--- a/solution.py
+++ b/solution.py
@@ -12,7 +12,7 @@
 MAXD = 128
 BLOCK = 256
 MESH = pl.DeviceIdType.MESH
-VMEM_BYTES = 40 * 1024 * 1024
+VMEM_BYTES = 60 * 1024 * 1024
 
 epsilon = 1e-06
 masked_score = -1e30
@@ -197,31 +197,6 @@
     return pl.CostEstimate(flops=flops, bytes_accessed=moved, transcendentals=special)
 
 
-def swap_experts(sizes, number, rows, values):
-    n = sizes["exp"]
-
-    def kernel(a_ref, b_ref, a_out, b_out, *sems):
-        greet(sizes, ["exp"])
-        one = Move(sizes, "exp", a_ref, a_out, sems[:3], split=True)
-        two = Move(sizes, "exp", b_ref, b_out, sems[3:], split=True)
-        start_all([two, one])
-        for m in (two, one):
-            m.wait()
-        for m in (two, one):
-            m.wait_sent()
-
-    return pl.pallas_call(
-        kernel,
-        out_shape=[jax.ShapeDtypeStruct(a.shape, a.dtype) for a in (rows, values)],
-        in_specs=any_space(2),
-        out_specs=any_space(2),
-        scratch_shapes=move_sems(n) + move_sems(n),
-        compiler_params=remote_params(number, 4 * 1024 * 1024),
-        cost_estimate=cost(0, 30_000_000),
-        name=f"swap_experts_{number}",
-    )(rows, values)
-
-
 def dot_nt(left, right):
     return lax.dot_general(
         left, right, (((1,), (1,)), ((), ())), preferred_element_type=jnp.float32
@@ -257,11 +232,13 @@
     return bias
 
 
-def first_keys(bounds_ref, start):
+def first_keys(lengths_ref, start):
     query = start + lax.broadcasted_iota(jnp.int32, (1, BLOCK), 1)
     first = jnp.zeros((1, BLOCK), jnp.int32)
+    bound = jnp.int32(0)
     for d in range(3):
-        first = jnp.where(query >= bounds_ref[d], bounds_ref[d], first)
+        bound = bound + lengths_ref[d]
+        first = jnp.where(query >= bound, bound, first)
     return first
 
 
@@ -336,7 +313,7 @@
     x_ref,
     g_ref,
     route_ref,
-    bounds_ref,
+    lengths_ref,
     w_ref,
     small_ref,
     proj_ref,
@@ -427,7 +404,7 @@
             vt_ref[:, at] = qkv_ref[c, 2 * size :, :]
         for i in range(blocks):
             qt = scaled_queries(qkv_ref, i, size)
-            first = first_keys(bounds_ref, i * BLOCK)
+            first = first_keys(lengths_ref, i * BLOCK)
             scores = []
             top = None
             for j in range(i + 1):
@@ -491,7 +468,7 @@
         m.wait_sent()
 
 
-def run_front(sizes, heads, experts, own_buckets, weight, small, proj, x, g, route_t, bounds):
+def run_front(sizes, heads, experts, own_buckets, weight, small, proj, x, g, route_t, lengths):
     n_ctx, n_exp = sizes["ctx"], sizes["exp"]
     rows, width = x.shape
     size = width // heads
@@ -536,27 +513,242 @@
         compiler_params=remote_params(1),
         cost_estimate=cost(60_000_000_000, 100_000_000, 2_400_000),
         name="run_front",
-    )(weight, small, proj, x, g, route_t, bounds)
-
-
-def backward_kernel(
+    )(weight, small, proj, x, g, route_t, lengths)
+
+
+def expert_kernel(
+    rows_ref, g_ref, gate_ref, up_ref, down_ref, out_ref, back_ref, dgate_ref, gup_ref, gdown_ref,
+    dy_ref, sum_out, sum_back,
+):
+    step = pl.program_id(0)
+    count, width = rows_ref.shape
+    sources = gate_ref.shape[0]
+    cap = count // sources
+
+    @pl.when(step == 0)
+    def _():
+        lanes = jnp.concatenate([gate_ref[s, 0:1, :] for s in range(sources)], axis=0)
+        columns = lanes.T
+        for s in range(sources):
+            at = slice(s * cap, (s + 1) * cap)
+            gate = columns[:cap, s : s + 1]
+            dy_ref[at, :] = (gate * g_ref[at, :].astype(jnp.float32)).astype(jnp.bfloat16)
+        sum_out[...] = jnp.zeros_like(sum_out)
+        sum_back[...] = jnp.zeros_like(sum_back)
+
+    rows, dy = rows_ref[...], dy_ref[...]
+    up, down = up_ref[0], down_ref[0]
+    x = dot_nt(rows, up)
+    c, a = math.sqrt(2.0 / math.pi), 0.044715
+    square = x * x
+    t = jnp.tanh(c * x * (1.0 + a * square))
+    half = 0.5 * (1.0 + t)
+    hidden = (x * half).astype(jnp.bfloat16)
+    slope = half + 0.5 * x * (1.0 - t * t) * (c * (1.0 + 3.0 * a * square))
+    dpre = (dot_nt(dy, down) * slope).astype(jnp.bfloat16)
+    gup_ref[...] = dot_tn(dpre, rows).astype(jnp.bfloat16)
+    gdown_ref[...] = dot_tn(hidden, dy).astype(jnp.bfloat16)
+    sum_out[...] += dot_nn(hidden, down)
+    sum_back[...] += dot_nn(dpre, up)
+
+    @pl.when(step == pl.num_programs(0) - 1)
+    def _():
+        back_ref[...] = sum_back[...].astype(jnp.bfloat16)
+        out = sum_out[...].astype(jnp.bfloat16)
+        out_ref[...] = out
+        dgate = jnp.sum(out.astype(jnp.float32) * g_ref[...].astype(jnp.float32), axis=1, keepdims=True)
+        lane = lax.broadcasted_iota(jnp.int32, (cap, 128), 1)
+        columns = jnp.zeros((cap, 128), jnp.float32)
+        for s in range(sources):
+            columns = jnp.where(lane == s, dgate[s * cap : (s + 1) * cap, :], columns)
+        turned = jnp.concatenate([columns] * (128 // cap), axis=0).T
+        for s in range(sources):
+            dgate_ref[s] = jnp.broadcast_to(turned[s : s + 1, :], (8, 128))
+
+
+def run_expert(rows, g, gates, weights):
+    count, width = rows.shape
+    hidden = weights.shape[1]
+    tile = 768
+    low, full = jnp.bfloat16, jnp.float32
+    whole = lambda shape: pl.BlockSpec(shape, lambda f: (0,) * len(shape))
+    return pl.pallas_call(
+        expert_kernel,
+        grid=(hidden // tile,),
+        out_shape=[
+            jax.ShapeDtypeStruct((count, width), low),
+            jax.ShapeDtypeStruct((count, width), low),
+            jax.ShapeDtypeStruct(gates.shape, full),
+            jax.ShapeDtypeStruct((hidden, width), low),
+            jax.ShapeDtypeStruct((hidden, width), low),
+        ],
+        in_specs=[
+            whole((count, width)),
+            whole((count, width)),
+            whole(gates.shape),
+            pl.BlockSpec((1, tile, width), lambda f: (0, f, 0)),
+            pl.BlockSpec((1, tile, width), lambda f: (1, f, 0)),
+        ],
+        out_specs=[
+            whole((count, width)),
+            whole((count, width)),
+            whole(gates.shape),
+            pl.BlockSpec((tile, width), lambda f: (f, 0)),
+            pl.BlockSpec((tile, width), lambda f: (f, 0)),
+        ],
+        scratch_shapes=[
+            pltpu.VMEM((count, width), low),
+            pltpu.VMEM((count, width), full),
+            pltpu.VMEM((count, width), full),
+        ],
+        compiler_params=pltpu.CompilerParams(vmem_limit_bytes=VMEM_BYTES),
+        cost_estimate=cost(14_500_000_000, 24_000_000, 1_600_000),
+        name="run_expert",
+    )(rows, g, gates, weights, weights)
+
+
+class RingSum:
+    def __init__(self, along_major, view, bufs, sems):
+        place = lax.axis_index("ctx")
+        major, minor = lax.div(place, 4), lax.rem(place, 4)
+        self.me = major if along_major else minor
+        self.device = (lambda k: k * 4 + minor) if along_major else (lambda k: major * 4 + k)
+        self.plus, self.minus = lax.rem(self.me + 1, 4), lax.rem(self.me + 3, 4)
+        self.far = lax.rem(self.me + 2, 4)
+        self.view = view
+        self.step, self.added, self.got, self.own = bufs
+        self.send_sem, self.recv_sem, self.own_sem = sems
+
+    def copy(self, k):
+        src, dst, peer = (
+            (lambda: self.view(self.far, 0), self.step.at[0], self.plus),
+            (lambda: self.view(self.far, 1), self.step.at[1], self.minus),
+            (lambda: self.view(self.plus, 1), self.got.at[0, 1], self.plus),
+            (lambda: self.view(self.minus, 0), self.got.at[1, 0], self.minus),
+            (lambda: self.added.at[0], self.got.at[0, 0], self.plus),
+            (lambda: self.added.at[1], self.got.at[1, 1], self.minus),
+        )[k]
+        return pltpu.make_async_remote_copy(
+            src_ref=src(),
+            dst_ref=dst,
+            send_sem=self.send_sem.at[k],
+            recv_sem=self.recv_sem.at[k],
+            device_id={"ctx": self.device(peer)},
+            device_id_type=MESH,
+        )
+
+    def local(self, k):
+        src, dst = (
+            (self.view(self.plus, 0), self.added.at[0]),
+            (self.view(self.minus, 1), self.added.at[1]),
+            (self.view(self.me, 0), self.own.at[0]),
+            (self.view(self.me, 1), self.own.at[1]),
+        )[k]
+        return pltpu.make_async_copy(src, dst, self.own_sem.at[k])
+
+    def start(self):
+        for k in range(4):
+            self.copy(k).start()
+        for k in range(4):
+            self.local(k).start()
+
+    def turn(self):
+        for k in range(2):
+            self.copy(k).wait_recv()
+            self.local(k).wait()
+            total = self.added[k].astype(jnp.float32) + self.step[k].astype(jnp.float32)
+            self.added[k] = total.astype(jnp.bfloat16)
+            self.copy(4 + k).start()
+
+    def wait(self):
+        for k in range(2, 4):
+            self.local(k).wait()
+        for k in range(2, 6):
+            self.copy(k).wait_recv()
+
+    def half(self, h, *at):
+        parts = (self.own[(h,) + at], self.got[(0, h) + at], self.got[(1, h) + at])
+        return sum(p.astype(jnp.float32) for p in parts)
+
+    def wait_sent(self):
+        for k in range(6):
+            self.copy(k).wait_send()
+
+
+def ring_space(shape):
+    low = jnp.bfloat16
+    return [
+        pltpu.VMEM((2,) + shape, low),
+        pltpu.VMEM((2,) + shape, low),
+        pltpu.VMEM((2, 2) + shape, low),
+        pltpu.VMEM((2,) + shape, low),
+    ]
+
+
+def ring_sems():
+    return [pltpu.SemaphoreType.DMA((6,)), pltpu.SemaphoreType.DMA((6,)), pltpu.SemaphoreType.DMA((4,))]
+
+
+def norm_back(x, gain, grad):
+    scale = lax.rsqrt(jnp.mean(x * x, axis=-1, keepdims=True) + epsilon)
+    scaled = grad * gain
+    inner = jnp.mean(scaled * x, axis=-1, keepdims=True)
+    grad_x = scale * scaled - x * (scale * scale * scale) * inner
+    return grad_x, jnp.sum(grad * x * scale, axis=0, keepdims=True)
+
+
+def summed(ref, count):
+    total = ref[0].astype(jnp.float32)
+    for s in range(1, count):
+        total = total + ref[s].astype(jnp.float32)
+    return total
+
+
+def middle_kernel(
     sizes,
     heads,
-    buckets,
-    do_in,
+    experts,
+    own_buckets,
+    back_in,
+    dgate_in,
     out_in,
-    terms_in,
+    up_in,
+    down_in,
+    info_ref,
+    g_ref,
+    mid_ref,
+    second_ref,
+    small_ref,
+    proj_ref,
+    mixed_ref,
     qkv_ref,
     stat_ref,
     table_ref,
-    bounds_ref,
+    lengths_ref,
     grad_out,
     out_out,
-    terms_out,
+    piece_ref,
     grad_ref,
     bias_ref,
+    dmid_ref,
+    part_ref,
+    up_sum,
+    down_sum,
+    back_got,
+    dgate_got,
+    do_sent,
     do_ref,
     sent_ref,
+    terms_sent,
+    terms_got,
+    up_a,
+    up_b,
+    up_c,
+    up_d,
+    down_a,
+    down_b,
+    down_c,
+    down_d,
     k_ref,
     v_ref,
     kt_ref,
@@ -569,18 +761,36 @@
     side_sum,
     *sems,
 ):
+    n_exp = sizes["exp"]
     parts, three, rows = qkv_ref.shape
     size = three // 3
+    width = heads * size
+    share = width // n_exp
     blocks = parts * rows // BLOCK
     half = BLOCK // 2
+    buckets = own_buckets * n_exp
+    cap = back_got.shape[1]
+    side = math.isqrt(parts)
     scale = 1.0 / math.sqrt(size)
-    greet(sizes, ["ctx", "exp"])
-    arrive = Move(sizes, "ctx", do_in, do_ref, sems[0:3], split=True, takers=heads)
-    back = Move(sizes, "ctx", sent_ref, grad_out, sems[3:6], split=True, senders=heads)
-    experts = Move(sizes, "exp", out_in, out_out, sems[6:9], split=True)
-    terms = Move(sizes, "exp", terms_in, terms_out, sems[9:12], split=True)
-    start_all([arrive])
-    start_all([experts, terms])
+    greet(sizes, ["exp", "ctx"])
+    returned = Move(sizes, "exp", back_in, back_got, sems[0:3], split=True)
+    gating = Move(sizes, "exp", dgate_in, dgate_got, sems[3:6], split=True)
+    outs = Move(sizes, "exp", out_in, out_out, sems[6:9], split=True)
+    terms = Move(sizes, "exp", terms_sent, terms_got, sems[9:12], split=True)
+    arrive = Move(sizes, "ctx", do_sent, do_ref, sems[12:15], split=True, takers=heads)
+    back = Move(sizes, "ctx", sent_ref, grad_out, sems[15:18], split=True, senders=heads)
+    ups = RingSum(
+        True, lambda k, h: up_in.at[k, pl.ds(2 * h, 2)], (up_a, up_b, up_c, up_d), sems[18:21]
+    )
+    downs = RingSum(
+        False,
+        lambda k, h: down_in.at[pl.ds(2 * h, 2), k],
+        (down_a, down_b, down_c, down_d),
+        sems[21:24],
+    )
+    start_all([gating, returned])
+    ups.start()
+    downs.start()
     is_head = lax.axis_index("ctx") < heads
 
     @pl.when(is_head)
@@ -597,6 +807,52 @@
             k_ref[at, :] = transposed(qkv_ref[c, size : 2 * size, :])
             v_ref[at, :] = transposed(qkv_ref[c, 2 * size :, :])
 
+    gates = [info_ref[c : c + 1, :] for c in range(2)]
+    slots = lax.broadcasted_iota(jnp.int32, (experts * cap, rows), 0).astype(jnp.float32)
+    hit = [slots == info_ref[2 + c : 3 + c, :] for c in range(2)]
+    expert = lax.broadcasted_iota(jnp.int32, (experts, rows), 0).astype(jnp.float32)
+    chosen = [(expert == info_ref[4 + c : 5 + c, :]).astype(jnp.float32) for c in range(2)]
+    begin = 2 + own_buckets
+    router = jnp.concatenate(
+        [small_ref[e, begin : begin + experts, :share] for e in range(n_exp)], axis=1
+    )
+    either = (hit[0] | hit[1]).astype(jnp.bfloat16)
+
+    gating.wait()
+    turned = jnp.concatenate([dgate_got[e, 0:1, :] for e in range(experts)], axis=0).T
+    column = jnp.concatenate([turned[:cap, e : e + 1] for e in range(experts)], axis=0)
+    dgate = [jnp.sum(jnp.where(hit[c], column, 0.0), axis=0, keepdims=True) for c in range(2)]
+    inner = gates[0] * dgate[0] + gates[1] * dgate[1]
+    dz = sum(chosen[c] * (gates[c] * (dgate[c] - inner)) for c in range(2))
+    dz_low = dz.astype(jnp.bfloat16)
+    dz_tall = jnp.concatenate([dz, jnp.zeros((rows - experts, rows), jnp.float32)], axis=0)
+    router_tall = jnp.concatenate(
+        [router, jnp.zeros((rows - experts, width), jnp.bfloat16)], axis=0
+    )
+    from_router = dot_nn(dz_tall.T.astype(jnp.bfloat16), router_tall)
+    part_ref[...] = jnp.zeros_like(part_ref)
+    part_ref[8 : 8 + experts, :] = dot_nn(dz_low, second_ref[...])
+
+    returned.wait()
+    start_all([outs])
+    dh = dot_tn(either, back_got[...].reshape(experts * cap, width)) + from_router
+    grad_mid, grad_gain = norm_back(mid_ref[...], full_row(small_ref, 1, share), dh)
+    grad_mid = g_ref[...].astype(jnp.float32) + grad_mid
+    dmid_ref[...] = grad_mid
+    part_ref[0:1, :] = grad_gain
+    low_mid = grad_mid.astype(jnp.bfloat16)
+    do_all = dot_nt(proj_ref[...].reshape(width, width), low_mid).astype(jnp.bfloat16)
+    for h in range(heads):
+        do_sent[h] = do_all[h * size : (h + 1) * size, :]
+    start_all([arrive])
+    terms_sent[...] = (
+        dot_nn(mixed_ref[...].reshape(width, rows), low_mid)
+        .astype(jnp.bfloat16)
+        .reshape(n_exp, share, width)
+    )
+    start_all([terms])
+    ups.turn()
+    downs.turn()
     arrive.wait()
 
     @pl.when(is_head)
@@ -605,7 +861,7 @@
         for i in range(blocks):
             qt = scaled_queries(qkv_ref, i, size)
             dot_ = jnp.concatenate([do_ref[2 * i], do_ref[2 * i + 1]], axis=1)
-            first = first_keys(bounds_ref, i * BLOCK)
+            first = first_keys(lengths_ref, i * BLOCK)
             stat = stat_ref[i : i + 1, :]
             probs, grads = [], []
             delta = jnp.zeros((1, BLOCK), jnp.float32)
@@ -637,7 +893,7 @@
             sent_ref[c, :size, :] = dq_ref[:, at]
             sent_ref[c, size : 2 * size, :] = dk_ref[:, at].astype(jnp.bfloat16)
             sent_ref[c, 2 * size :, :] = dv_ref[:, at].astype(jnp.bfloat16)
-        bias_ref[0:1, :] = far
+        bias_ref[0:1, :] = far[:, :half] + far[:, half:]
 
     start_all([back])
 
@@ -646,9 +902,8 @@
         grad_ref[:size, :] = dq_ref[...]
         grad_ref[size : 2 * size, :] = dk_ref[...].astype(jnp.bfloat16)
         grad_ref[2 * size :, :] = dv_ref[...].astype(jnp.bfloat16)
-        far = bias_ref[0:1, :] + jnp.sum(side_sum[:half, :], axis=0, keepdims=True)
-        far_half = jnp.sum(side_sum[half:, half:], axis=0, keepdims=True)
-        far = far + jnp.concatenate([jnp.zeros_like(far_half), far_half], axis=1)
+        far = bias_ref[0:1, :] + jnp.sum(side_sum[:half, :half], axis=0, keepdims=True)
+        far = far + jnp.sum(side_sum[:, half:], axis=0, keepdims=True)
         diag_bucket = near_buckets(buckets, 0, BLOCK, BLOCK)
         side_bucket = near_buckets(buckets, half, half, half)
         for b in range(buckets):
@@ -656,38 +911,66 @@
             two = jnp.sum(
                 jnp.where(side_bucket == b, side_sum[half:, :half], 0.0), axis=0, keepdims=True
             )
-            row = one + jnp.concatenate([two, jnp.zeros_like(two)], axis=1)
+            row = one[:, :half] + one[:, half:] + two
             if b == buckets - 1:
                 row = row + far
             bias_ref[b : b + 1, :] = row
 
-    experts.wait()
     terms.wait()
+    total = summed(terms_got, n_exp).astype(jnp.bfloat16)
+    for t in range(piece_ref.shape[0]):
+        piece_ref[t] = total[t * 16 : (t + 1) * 16, :]
+    ups.wait()
+    downs.wait()
+    for k in range(side):
+        up_sum[k] = ups.half(k // 2, k % 2).astype(jnp.bfloat16)
+        down_sum[k] = downs.half(k // 2, k % 2).astype(jnp.bfloat16)
+    outs.wait()
     back.wait()
-    for m in (arrive, back, experts, terms):
+    for m in (returned, gating, outs, terms, arrive, back, ups, downs):
         m.wait_sent()
 
 
-def attention_backward(sizes, do, expert_out, terms, qkv, stat, table, bounds):
+def run_middle(
+    sizes, heads, experts, own_buckets, expert_back, dgate, expert_out, up_terms, down_terms, info,
+    g, mid, second, dense, proj, mixed, qkv, stat, table, lengths,
+):
     n_ctx, n_exp = sizes["ctx"], sizes["exp"]
-    heads, size, rows = do.shape
-    buckets = table.shape[0]
+    rows, width = mid.shape
+    size = width // heads
     seq = n_ctx * rows
+    share = width // n_exp
+    side = math.isqrt(n_ctx)
     low, full = jnp.bfloat16, jnp.float32
+    chunk = up_terms.shape[0] // n_ctx
+    square = (side, side, chunk, width)
+    assert n_ctx == 16 and experts == 8 and rows == 128
     return pl.pallas_call(
-        functools.partial(backward_kernel, sizes, heads, buckets),
+        functools.partial(middle_kernel, sizes, heads, experts, own_buckets),
         out_shape=[
             jax.ShapeDtypeStruct((heads, 3 * size, rows), low),
             jax.ShapeDtypeStruct(expert_out.shape, low),
-            jax.ShapeDtypeStruct(terms.shape, low),
+            jax.ShapeDtypeStruct((share // 16, 16, width), low),
             jax.ShapeDtypeStruct((3 * size, seq), low),
-            jax.ShapeDtypeStruct((buckets, BLOCK), full),
+            jax.ShapeDtypeStruct(table.shape, full),
+            jax.ShapeDtypeStruct((rows, width), full),
+            jax.ShapeDtypeStruct((16, width), full),
+            jax.ShapeDtypeStruct((side, chunk, width), low),
+            jax.ShapeDtypeStruct((side, chunk, width), low),
         ],
-        in_specs=any_space(3) + in_vmem(3) + in_smem(1),
-        out_specs=any_space(3) + in_vmem(2),
+        in_specs=in_vmem(2) + any_space(3) + in_vmem(10) + in_smem(1),
+        out_specs=in_vmem(1) + any_space(1) + in_vmem(7),
         scratch_shapes=[
+            pltpu.VMEM(expert_back.shape, low),
+            pltpu.VMEM(dgate.shape, full),
+            pltpu.VMEM((heads, size, rows), low),
             pltpu.VMEM((n_ctx, size, rows), low),
             pltpu.VMEM((n_ctx, 3 * size, rows), low),
+            pltpu.VMEM((n_exp, share, width), low),
+            pltpu.VMEM((n_exp, share, width), low),
+        ]
+        + ring_space((2, chunk, width)) * 2
+        + [
             pltpu.VMEM((seq, size), low),
             pltpu.VMEM((seq, size), low),
             pltpu.VMEM((size, seq), low),
@@ -699,237 +982,251 @@
             pltpu.VMEM((BLOCK, BLOCK), full),
             pltpu.VMEM((BLOCK, BLOCK), full),
         ]
-        + move_sems(n_ctx)
-        + move_sems(n_ctx)
-        + move_sems(n_exp)
-        + move_sems(n_exp),
-        compiler_params=remote_params(3),
-        cost_estimate=cost(20_000_000_000, 60_000_000, 2_400_000),
-        name="attention_backward",
-    )(do, expert_out, terms, qkv, stat, table, bounds)
-
-
-def expert_kernel(
-    rows_ref, g_ref, gate_ref, up_ref, down_ref, out_ref, back_ref, dgate_ref, wg_ref,
-    dy_ref, sum_out, sum_back,
+        + move_sems(n_exp) * 4
+        + move_sems(n_ctx) * 2
+        + ring_sems() * 2,
+        compiler_params=remote_params(2),
+        cost_estimate=cost(60_000_000_000, 100_000_000, 2_400_000),
+        name="run_middle",
+    )(
+        expert_back, dgate, expert_out, up_terms.reshape(square), down_terms.reshape(square), info,
+        g, mid, second, dense, proj, mixed, qkv, stat, table, lengths,
+    )
+
+
+def last_kernel(
+    sizes, heads, experts, own_buckets,
+    grad_ref, w_ref, x_ref, small_ref, dmid_ref, turned_ref, h_ref, bias_ref, part_ref, piece_in,
+    out_ref, mid_ref, info_ref, up_in, down_in,
+    in_out, block_out, head_all, small_all, piece_all, up_c, up_d, down_c, down_d,
+    head_in, small_in, dqkv_ref, head_parts, small_parts, piece_parts, head_sent, small_sent,
+    piece_sent, up_a, up_b, down_a, down_b, *sems,
 ):
-    step = pl.program_id(0)
-    count, width = rows_ref.shape
-    sources = gate_ref.shape[0]
-    cap = count // sources
-
-    @pl.when(step == 0)
-    def _():
-        lanes = jnp.concatenate([gate_ref[s, 0:1, :] for s in range(sources)], axis=0)
-        columns = lanes.T
-        for s in range(sources):
-            at = slice(s * cap, (s + 1) * cap)
-            gate = columns[:cap, s : s + 1]
-            dy_ref[at, :] = (gate * g_ref[at, :].astype(jnp.float32)).astype(jnp.bfloat16)
-        sum_out[...] = jnp.zeros_like(sum_out)
-        sum_back[...] = jnp.zeros_like(sum_back)
-
-    rows, dy = rows_ref[...], dy_ref[...]
-    up, down = up_ref[0], down_ref[0]
-    x = dot_nt(rows, up)
-    c, a = math.sqrt(2.0 / math.pi), 0.044715
-    square = x * x
-    t = jnp.tanh(c * x * (1.0 + a * square))
-    half = 0.5 * (1.0 + t)
-    hidden = (x * half).astype(jnp.bfloat16)
-    slope = half + 0.5 * x * (1.0 - t * t) * (c * (1.0 + 3.0 * a * square))
-    dpre = (dot_nt(dy, down) * slope).astype(jnp.bfloat16)
-    wg_ref[:, :width] = dot_tn(dpre, rows).astype(jnp.bfloat16)
-    wg_ref[:, width:] = dot_tn(hidden, dy).astype(jnp.bfloat16)
-    sum_out[...] += dot_nn(hidden, down)
-    sum_back[...] += dot_nn(dpre, up)
-
-    @pl.when(step == pl.num_programs(0) - 1)
-    def _():
-        back_ref[...] = sum_back[...].astype(jnp.bfloat16)
-        out = sum_out[...].astype(jnp.bfloat16)
-        out_ref[...] = out
-        dgate = jnp.sum(out.astype(jnp.float32) * g_ref[...].astype(jnp.float32), axis=1, keepdims=True)
-        lane = lax.broadcasted_iota(jnp.int32, (cap, 128), 1)
-        columns = jnp.zeros((cap, 128), jnp.float32)
-        for s in range(sources):
-            columns = jnp.where(lane == s, dgate[s * cap : (s + 1) * cap, :], columns)
-        turned = jnp.concatenate([columns] * (128 // cap), axis=0).T
-        for s in range(sources):
-            dgate_ref[s] = jnp.broadcast_to(turned[s : s + 1, :], (8, 128))
-
-
-def run_expert(rows, g, gates, weights):
-    count, width = rows.shape
-    hidden = weights.shape[1]
-    tile = 256
-    low, full = jnp.bfloat16, jnp.float32
-    whole = lambda shape: pl.BlockSpec(shape, lambda f: (0,) * len(shape))
-    return pl.pallas_call(
-        expert_kernel,
-        grid=(hidden // tile,),
-        out_shape=[
-            jax.ShapeDtypeStruct((count, width), low),
-            jax.ShapeDtypeStruct((count, width), low),
-            jax.ShapeDtypeStruct(gates.shape, full),
-            jax.ShapeDtypeStruct((hidden, 2 * width), low),
-        ],
-        in_specs=[
-            whole((count, width)),
-            whole((count, width)),
-            whole(gates.shape),
-            pl.BlockSpec((1, tile, width), lambda f: (0, f, 0)),
-            pl.BlockSpec((1, tile, width), lambda f: (1, f, 0)),
-        ],
-        out_specs=[
-            whole((count, width)),
-            whole((count, width)),
-            whole(gates.shape),
-            pl.BlockSpec((tile, 2 * width), lambda f: (f, 0)),
-        ],
-        scratch_shapes=[
-            pltpu.VMEM((count, width), low),
-            pltpu.VMEM((count, width), full),
-            pltpu.VMEM((count, width), full),
-        ],
-        compiler_params=pltpu.CompilerParams(vmem_limit_bytes=VMEM_BYTES),
-        cost_estimate=cost(14_500_000_000, 24_000_000, 1_600_000),
-        name="run_expert",
-    )(rows, g, gates, weights, weights)
-
-
-def total_kernel(
-    sizes, heads, takers, head_in, small_in, out_in, qkv_out, weight_out, small_out, table_out,
-    head_parts, small_parts, out_parts, head_sent, small_sent, out_sent,
-    head_all, small_all, out_all, *sems,
-):
-    share, three = head_in.shape[1:]
-    size = three // 3
+    n_ctx, n_exp = sizes["ctx"], sizes["exp"]
+    takers, sixteen, width = piece_in.shape
+    rows = x_ref.shape[0]
+    size = width // heads
+    share = width // n_exp
     half = share // 2
-    width = heads * size
-    sixteen = out_sent.shape[0]
     me = lax.axis_index("ctx")
-    greet(sizes, ["ctx", "exp"])
+    greet(sizes, ["exp", "ctx"])
     first = [
         Move(sizes, "exp", head_in, head_parts, sems[0:3], split=True),
         Move(sizes, "exp", small_in, small_parts, sems[3:6], split=True),
-        Move(sizes, "ctx", out_in, out_parts, sems[6:9], split=True, takers=takers),
+        Move(sizes, "ctx", piece_in, piece_parts, sems[6:9], split=True, takers=takers),
     ]
     second = [
         Move(sizes, "ctx", head_sent, head_all, sems[9:12], senders=heads),
         Move(sizes, "ctx", small_sent, small_all, sems[12:15]),
-        Move(sizes, "ctx", out_sent, out_all, sems[15:18], senders=takers),
+        Move(sizes, "ctx", piece_sent, piece_all, sems[15:18], senders=takers),
     ]
-    start_all(first)
+    part_rows = up_d.shape[1]
+    ups = RingSum(
+        False,
+        lambda k, h: up_in.at[k, pl.ds(h * part_rows, part_rows)],
+        (up_a, up_b, up_c, up_d),
+        sems[18:21],
+    )
+    downs = RingSum(
+        True,
+        lambda k, h: down_in.at[k, pl.ds(h * part_rows, part_rows)],
+        (down_a, down_b, down_c, down_d),
+        sems[21:24],
+    )
+    start_all(first[2:])
+
+    @pl.when(me < heads)
+    def _():
+        terms = dot_nn(turned_ref[...], h_ref[...]).T.astype(jnp.bfloat16)
+        for e in range(n_exp):
+            head_in[e] = terms[e * share : (e + 1) * share, :]
+
+    start_all(first[:1])
+    ups.start()
+    downs.start()
+
+    for part in range(3):
+        for pair in range(heads // 2):
+            both = jnp.concatenate(
+                [
+                    grad_ref[2 * pair + k, part * size : (part + 1) * size, :]
+                    for k in range(2)
+                ],
+                axis=0,
+            )
+            at = part * width + 2 * size * pair
+            dqkv_ref[:, at : at + 2 * size] = transposed(both)
+    dh = jnp.zeros((rows, width), jnp.float32)
+    for at in range(0, 3 * width, 256):
+        piece = w_ref[:, :, at : at + 256].reshape(width, 256)
+        dh = dh + dot_nt(dqkv_ref[:, at : at + 256], piece)
+    x = x_ref[...].astype(jnp.float32)
+    grad_x, grad_gain = norm_back(x, full_row(small_ref, 0, share), dh)
+    in_out[...] = dmid_ref[...] + grad_x
+
+    bias = jnp.sum(bias_ref[...], axis=1, keepdims=True)
+    small_in[...] = jnp.zeros_like(small_in)
+    for e in range(n_exp):
+        at = slice(e * share, (e + 1) * share)
+        small_in[e, 0:1, :share] = grad_gain[:, at]
+        small_in[e, 1:2, :share] = part_ref[0:1, at]
+        small_in[e, 2 : 2 + experts, :share] = part_ref[8 : 8 + experts, at]
+        small_in[e, 2 + experts : 2 + experts + own_buckets, :] = jnp.broadcast_to(
+            bias[e * own_buckets : (e + 1) * own_buckets, :], (own_buckets, 128)
+        )
+    start_all(first[1:2])
+    ups.turn()
+    downs.turn()
+
     first[0].wait()
-    total = head_parts[0].astype(jnp.float32)
-    for s in range(1, sizes["exp"]):
-        total = total + head_parts[s].astype(jnp.float32)
-    total = total.astype(jnp.bfloat16)
+    total = summed(head_parts, n_exp).astype(jnp.bfloat16)
     head_sent[:share, :] = total[:, : 2 * size]
     head_sent[share:, :] = jnp.concatenate(
         [total[:half, 2 * size :], total[half:, 2 * size :]], axis=1
     )
     start_all(second[:1])
-    first[1].wait()
-    little = small_parts[0]
-    for s in range(1, sizes["exp"]):
-        little = little + small_parts[s]
-    small_sent[...] = little
-    start_all(second[1:2])
     first[2].wait()
 
     @pl.when(me < takers)
     def _():
-        weight = out_parts[0].astype(jnp.float32)
-        for s in range(1, sizes["ctx"]):
-            weight = weight + out_parts[s].astype(jnp.float32)
-        out_sent[...] = weight.astype(jnp.bfloat16)
+        piece_sent[...] = summed(piece_parts, n_ctx).astype(jnp.bfloat16)
 
     start_all(second[2:])
-    second[0].wait()
+    first[1].wait()
+    small_sent[...] = summed(small_parts, n_exp)
+    start_all(second[1:2])
+
+    slots = lax.broadcasted_iota(jnp.int32, (experts * rows // 2, rows), 0).astype(jnp.float32)
+    hit = [(slots == info_ref[2 + c : 3 + c, :]).astype(jnp.bfloat16) for c in range(2)]
+    both = jnp.concatenate(hit, axis=1)
+    picked = dot_tn(both, out_ref[...].reshape(experts * rows // 2, width))
+    tall = jnp.concatenate([info_ref[...], jnp.zeros((rows - 8, rows), jnp.float32)], axis=0).T
+    mixed = mid_ref[...] + (tall[:, 0:1] * picked[:rows] + tall[:, 1:2] * picked[rows:])
+    block_out[...] = mixed.astype(jnp.bfloat16)
+
+    ups.wait()
+    downs.wait()
+    for m in second:
+        m.wait()
+    for m in first + second + [ups, downs]:
+        m.wait_sent()
+
+
+def run_last(
+    sizes, heads, experts, own_buckets, grad_qkv, weight, x, dense, dmid, turned, h_all, bias,
+    parts, pieces, returned, mid, info, up_sum, down_sum,
+):
+    n_ctx, n_exp = sizes["ctx"], sizes["exp"]
+    rows, width = x.shape
+    size = width // heads
+    share = width // n_exp
+    takers, sixteen, _ = pieces.shape
+    side, chunk, _ = up_sum.shape
+    low, full = jnp.bfloat16, jnp.float32
+    assert 2 + experts + own_buckets <= 16
+    return pl.pallas_call(
+        functools.partial(last_kernel, sizes, heads, experts, own_buckets),
+        out_shape=[
+            jax.ShapeDtypeStruct((rows, width), full),
+            jax.ShapeDtypeStruct((rows, width), low),
+            jax.ShapeDtypeStruct((heads, share * 3 // 2, 128), low),
+            jax.ShapeDtypeStruct((n_ctx, 16, 128), full),
+            jax.ShapeDtypeStruct((takers, sixteen, width), low),
+        ]
+        + [
+            jax.ShapeDtypeStruct((2, 2, chunk // 2, width), low),
+            jax.ShapeDtypeStruct((2, chunk // 2, width), low),
+        ]
+        * 2,
+        in_specs=in_vmem(15),
+        out_specs=in_vmem(9),
+        scratch_shapes=[
+            pltpu.VMEM((n_exp, share, 3 * size), low),
+            pltpu.VMEM((n_exp, 16, 128), full),
+            pltpu.VMEM((rows, 3 * width), low),
+            pltpu.VMEM((n_exp, share, 3 * size), low),
+            pltpu.VMEM((n_exp, 16, 128), full),
+            pltpu.VMEM((n_ctx, sixteen, width), low),
+            pltpu.VMEM((share * 3 // 2, 128), low),
+            pltpu.VMEM((16, 128), full),
+            pltpu.VMEM((sixteen, width), low),
+        ]
+        + ring_space((chunk // 2, width))[:2] * 2
+        + move_sems(n_exp) * 2
+        + move_sems(n_ctx) * 4
+        + ring_sems() * 2,
+        compiler_params=remote_params(3),
+        cost_estimate=cost(4_000_000_000, 60_000_000),
+        name="run_last",
+    )(
+        grad_qkv, weight, x, dense, dmid, turned, h_all, bias, parts, pieces, returned, mid, info,
+        up_sum, down_sum,
+    )
+
+
+def finish_kernel(
+    sizes, experts, in_ref, block_ref, head_ref, small_ref, piece_ref, up_got, up_own, down_got,
+    down_own, block_out, in_out, one_out, two_out, qkv_out, weight_out, router_out, table_out,
+    up_out, down_out,
+):
+    heads = head_ref.shape[0]
+    share, width = weight_out.shape
+    size = width // heads
+    half = share // 2
+    own_buckets = table_out.shape[0]
+    block_out[0] = block_ref[...]
+    in_out[0] = in_ref[...]
     for h in range(heads):
-        got = head_all[h].astype(jnp.float32)
+        got = head_ref[h].astype(jnp.float32)
         at = h * size
         qkv_out[:, at : at + size] = got[:share, :size]
         qkv_out[:, width + at : width + at + size] = got[:share, size:]
         qkv_out[:half, 2 * width + at : 2 * width + at + size] = got[share:, :size]
         qkv_out[half:, 2 * width + at : 2 * width + at + size] = got[share:, size:]
-    second[1].wait()
-    sums = small_all[0]
-    for s in range(1, sizes["ctx"]):
-        sums = sums + small_all[s]
-    small_out[...] = sums
-    for h in range(heads):
-        table_out[h : h + 1, :] = small_all[h, 0:1, :]
-    second[2].wait()
-    for s in range(takers):
-        weight_out[s * sixteen : (s + 1) * sixteen, :] = out_all[s].astype(jnp.float32)
-    for m in first + second:
-        m.wait_sent()
-
-
-def total_dense(sizes, heads, head_terms, small, out_terms):
-    n_ctx, n_exp = sizes["ctx"], sizes["exp"]
-    _, share, three = head_terms.shape
-    takers, sixteen, width = out_terms.shape
+    takers, sixteen, _ = piece_ref.shape
+    for t in range(takers):
+        weight_out[t * sixteen : (t + 1) * sixteen, :] = piece_ref[t].astype(jnp.float32)
+    sums = summed(small_ref, sizes["ctx"])
+    one_out[...] = sums[0:1, :share]
+    two_out[...] = sums[1:2, :share]
+    router_out[...] = sums[2 : 2 + experts, :share]
+    begin = 2 + experts
+    table_out[...] = jnp.concatenate(
+        [small_ref[h, begin : begin + own_buckets, 0:1] for h in range(heads)], axis=1
+    )
+    for got, own, out in ((up_got, up_own, up_out), (down_got, down_own, down_out)):
+        rows = own.shape[1]
+        for h in range(2):
+            out[0, h * rows : (h + 1) * rows, :] = sum(
+                p.astype(jnp.float32) for p in (own[h], got[0, h], got[1, h])
+            )
+
+
+def finish(sizes, heads, experts, own_buckets, parts):
+    rows, width = parts[0].shape
+    share = width // sizes["exp"]
+    chunk = 2 * parts[-1].shape[1]
     low, full = jnp.bfloat16, jnp.float32
     return pl.pallas_call(
-        functools.partial(total_kernel, sizes, heads, takers),
+        functools.partial(finish_kernel, sizes, experts),
         out_shape=[
+            jax.ShapeDtypeStruct((1, rows, width), low),
+            jax.ShapeDtypeStruct((1, rows, width), full),
+            jax.ShapeDtypeStruct((1, share), full),
+            jax.ShapeDtypeStruct((1, share), full),
             jax.ShapeDtypeStruct((share, 3 * width), full),
             jax.ShapeDtypeStruct((share, width), full),
-            jax.ShapeDtypeStruct(small.shape[1:], full),
-            jax.ShapeDtypeStruct((heads, 128), full),
+            jax.ShapeDtypeStruct((experts, share), full),
+            jax.ShapeDtypeStruct((own_buckets, heads), full),
+            jax.ShapeDtypeStruct((1, chunk, width), full),
+            jax.ShapeDtypeStruct((1, chunk, width), full),
         ],
-        in_specs=in_vmem(3),
-        out_specs=in_vmem(4),
-        scratch_shapes=[
-            pltpu.VMEM(head_terms.shape, low),
-            pltpu.VMEM(small.shape, full),
-            pltpu.VMEM((n_ctx, sixteen, width), low),
-            pltpu.VMEM((share * 3 // 2, 128), low),
-            pltpu.VMEM(small.shape[1:], full),
-            pltpu.VMEM((sixteen, width), low),
-            pltpu.VMEM((heads, share * 3 // 2, 128), low),
-            pltpu.VMEM((n_ctx,) + small.shape[1:], full),
-            pltpu.VMEM((takers, sixteen, width), low),
-        ]
-        + move_sems(n_exp)
-        + move_sems(n_exp)
-        + move_sems(n_ctx)
-        + move_sems(n_ctx)
-        + move_sems(n_ctx)
-        + move_sems(n_ctx),
-        compiler_params=remote_params(4),
-        cost_estimate=cost(0, 60_000_000),
-        name="total_dense",
-    )(head_terms, small, out_terms)
-
-
-def split_kernel(both_ref, up_ref, down_ref):
-    width = up_ref.shape[1]
-    up_ref[...] = both_ref[:, :width].astype(jnp.float32)
-    down_ref[...] = both_ref[:, width:].astype(jnp.float32)
-
-
-def split_weights(both):
-    rows, width = both.shape[0], both.shape[1] // 2
-    return pl.pallas_call(
-        split_kernel,
-        out_shape=[jax.ShapeDtypeStruct((rows, width), jnp.float32)] * 2,
-        in_specs=in_vmem(1),
-        out_specs=in_vmem(2),
-        compiler_params=pltpu.CompilerParams(vmem_limit_bytes=8 * 1024 * 1024),
-        cost_estimate=cost(0, 2_000_000),
-        name="split_weights",
-    )(both)
-
-
-def rms_scale(values, gain_row):
-    return (
-        values * lax.rsqrt(jnp.mean(values * values, axis=-1, keepdims=True) + epsilon) * gain_row
-    )
+        in_specs=in_vmem(len(parts)),
+        out_specs=in_vmem(10),
+        compiler_params=pltpu.CompilerParams(vmem_limit_bytes=VMEM_BYTES),
+        cost_estimate=cost(0, 8_000_000),
+        name="finish",
+    )(*parts)
 
 
 def local(
@@ -950,15 +1247,10 @@
     low, full = jnp.bfloat16, jnp.float32
     n_ctx, n_exp = sizes["ctx"], sizes["exp"]
     rows, width = block_in.shape[1:]
-    seq_len = rows * n_ctx
     share = width // n_exp
     own_buckets, heads = bias_table.shape
-    buckets = own_buckets * n_exp
-    size = width // heads
     experts = routing_weight.shape[1]
-    x_in = block_in[0].astype(full)
     g_low = cotangent[0]
-    grad_out = g_low.astype(full)
 
     expert_weights = lax.all_gather(
         jnp.concatenate([up_weight, down_weight], axis=0), "ctx", axis=1, tiled=True
@@ -972,7 +1264,7 @@
     small = jnp.pad(small, ((0, -small.shape[0] % 16), (0, 0)))
     capacity = min(rows, 4 * rows // experts)
     piece = (experts, capacity, width)
-    bounds = jnp.cumsum(doc_lengths[0]).astype(jnp.int32)
+    lengths = doc_lengths[0]
     (
         qkv_full,
         dense,
@@ -999,103 +1291,63 @@
         block_in[0],
         g_low,
         routes[0].T,
-        bounds,
+        lengths,
     )
     h_all = lax.all_gather(h_first, "ctx", axis=0, tiled=True)
-    qkv_full = qkv_full.reshape(width, 3 * width)
-    proj_full = proj_full.reshape(width, width)
-    attended_t = mixed.reshape(width, rows)
-    gain_one = dense[:, 0, :share].reshape(width).astype(full)
-    gain_two = dense[:, 1, :share].reshape(width).astype(full)
-    router_t = dense[:, 2 + own_buckets : 2 + own_buckets + experts, :share]
-    router_t = jnp.transpose(router_t, (1, 0, 2)).reshape(experts, width)
-    gates = info[:2].T
-    slots = jnp.arange(experts * capacity, dtype=jnp.int32).astype(full)
-    found = [info[2 + c][:, None] == slots[None, :] for c in range(2)]
-    choose = (routes[0][:, :, None] == jnp.arange(experts, dtype=jnp.int32)).astype(full)
-    expert_out, expert_back, dgate, weight_terms = run_expert(
+    expert_out, expert_back, dgate, up_terms, down_terms = run_expert(
         expert_rows.reshape(experts * capacity, width),
         g_rows.reshape(experts * capacity, width),
         gate_rows,
         expert_weights,
     )
-    h_all, weight_terms = lax.optimization_barrier((h_all, weight_terms))
-    weight_grads = lax.psum_scatter(weight_terms, "ctx", scatter_dimension=0, tiled=True)
-    grad_back, dgate = swap_experts(sizes, 6, expert_back.reshape(piece), dgate)
-
-    grad_back = grad_back.reshape(experts * capacity, width)
-    dgate = dgate[:, 0, :capacity].reshape(1, experts * capacity)
-    grad_gates = jnp.stack(
-        [jnp.sum(jnp.where(found[c], dgate, 0.0), axis=1) for c in range(2)], axis=-1
-    )
-    grad_chosen = gates * (grad_gates - jnp.sum(gates * grad_gates, axis=-1, keepdims=True))
-    grad_logits = jnp.sum(choose * grad_chosen[:, :, None], axis=1).astype(low)
-    grad_h_second = jnp.dot(
-        (found[0] | found[1]).astype(low), grad_back, preferred_element_type=full
-    ) + jnp.dot(grad_logits, router_t, preferred_element_type=full)
-    grad_x_norm, grad_gain_two = jax.vjp(rms_scale, x_mid, gain_two)[1](grad_h_second)
-    grad_x_mid = grad_out + grad_x_norm
-    grad_proj = grad_x_mid.astype(low)
-    grad_attended = dot_nt(proj_full, grad_proj).astype(low).reshape(heads, size, rows)
-    out_terms = jnp.dot(attended_t, grad_proj, preferred_element_type=full).astype(low)
-
-    grad_qkv_t, returned, out_parts, grad_head, bias_rows = attention_backward(
+    grad_qkv_t, returned, pieces, grad_head, bias_rows, grad_mid, parts, up_sum, down_sum = (
+        run_middle(
+            sizes,
+            heads,
+            experts,
+            own_buckets,
+            expert_back.reshape(piece),
+            dgate,
+            expert_out.reshape(piece),
+            up_terms,
+            down_terms,
+            info,
+            g_low,
+            x_mid,
+            h_second,
+            dense,
+            proj_full,
+            mixed,
+            qkv_head,
+            stat,
+            table_head,
+            lengths,
+        )
+    )
+    last = run_last(
         sizes,
-        grad_attended,
-        expert_out.reshape(piece),
-        out_terms.reshape(n_exp, share, width),
-        qkv_head,
-        stat,
-        table_head,
-        bounds,
-    )
-    grad_qkv_t = jnp.transpose(
-        grad_qkv_t.reshape(heads, 3, size, rows), (1, 0, 2, 3)
-    ).reshape(3 * width, rows)
-    grad_h_first = lax.dot_general(
-        grad_qkv_t, qkv_full, (((0,), (1,)), ((), ())), preferred_element_type=full
-    )
-    grad_x_first, grad_gain_one = jax.vjp(rms_scale, x_in, gain_one)[1](grad_h_first)
-    grad_in = (grad_x_mid + grad_x_first)[None]
-    grad_router = dot_tn(grad_logits, h_second).reshape(experts, n_exp, share)
-    head_terms = (
-        lax.dot_general(h_all, grad_head, (((0,), (1,)), ((), ())), preferred_element_type=full)
-        .astype(low)
-        .reshape(n_exp, share, 3 * size)
-    )
-    bias_part = jnp.sum(bias_rows, axis=1).reshape(n_exp, own_buckets)
-    first_row = jnp.concatenate([grad_gain_one.reshape(n_exp, share), bias_part], axis=1)
-    totals = jnp.concatenate(
-        [
-            lanes(first_row)[:, None, :],
-            lanes(grad_gain_two.reshape(n_exp, share))[:, None, :],
-            jnp.pad(jnp.transpose(grad_router, (1, 0, 2)), ((0, 0), (0, 0), (0, 128 - share))),
-        ],
-        axis=1,
-    )
-    totals = jnp.pad(totals, ((0, 0), (0, -totals.shape[1] % 8), (0, 0)))
-    out_sum = jnp.sum(out_parts.astype(full), axis=0).astype(low).reshape(share // 16, 16, width)
-    grad_qkv, grad_out_weight, sums, table_rows = total_dense(
-        sizes, heads, head_terms, totals, out_sum
-    )
-    returned = returned.reshape(experts * capacity, width)
-    picked = jnp.dot(
-        jnp.concatenate(found, axis=0).astype(low), returned, preferred_element_type=full
-    )
-    block_out = x_mid + (gates[:, :1] * picked[:rows] + gates[:, 1:] * picked[rows:])
-    grad_up, grad_down = split_weights(weight_grads)
-    return (
-        block_out.astype(low)[None],
-        grad_in,
-        sums[0, :share],
-        sums[1, :share],
-        grad_qkv,
-        grad_out_weight,
-        sums[2 : 2 + experts, :share].T,
-        table_rows[:, share : share + own_buckets].T,
-        grad_up[None],
-        grad_down[None],
-    )
+        heads,
+        experts,
+        own_buckets,
+        grad_qkv_t,
+        qkv_full,
+        block_in[0],
+        dense,
+        grad_mid,
+        grad_head,
+        h_all,
+        bias_rows,
+        parts,
+        pieces,
+        returned,
+        x_mid,
+        info,
+        up_sum,
+        down_sum,
+    )
+    out = finish(sizes, heads, experts, own_buckets, last)
+    block_out, grad_in, one, two, qkv, proj, router, *rest = out
+    return (block_out, grad_in, one[0], two[0], qkv, proj, router.T, *rest)
 
 
 def solution(mesh):

time: 274 us -> 238 us (0.87)
  local copies, waits for them, and re-layouts: 30.7 us -> 0.6 us
  Pallas kernels: 184 us -> 210 us
  matrix products: 12 us -> 0 us
  waiting for transfers between devices: 19.4 us -> 8.58 us
  other arithmetic: 12.5 us -> 2.64 us
    pallas_call x4 -> x3, Pallas kernels: 85.8 us -> 112 us  [the longest x1 72.9 us: run_middle(): pl.pallas_call(functools.partial(middle_kernel, sizes, heads, experts, ow...]
    unnamed x99 -> x0, local copies, waits for them, and re-layouts: 23.2 us -> none
    all_gather x1, waiting for transfers between devices: 17.1 us -> 0.02 us  [local(): h_all = lax.all_gather(h_first, 'ctx', axis=0, tiled=True)]
    dot_general x8 -> x0, matrix products: 12 us -> none  [the longest x1 3.42 us: local(): lax.dot_general(h_all, grad_head, (((0,), (1,)), ((), ())), preferred_ele...]
    all_gather x1, waiting for transfers between devices: 2.17 us -> 8.53 us  [local(): lax.all_gather(jnp.concatenate([up_weight, down_weight], axis=0), 'ctx',...]
    reshape x7 -> x0, local copies, waits for them, and re-layouts: 3.71 us -> none  [the longest x1 1.33 us: local(): bias_part = jnp.sum(bias_rows, axis=1).reshape(n_exp, own_buckets)]
  transfers between devices with their start and end apart: 3 -> 2, of which waited for: 2 -> 1; matrix products, arithmetic and copies ran while one was open for 11% -> 1% of each run, Pallas kernels for 67% -> 72%
where the time goes in v2:
time: 238 us; the launch traced here: 236 us
  Pallas kernels  210 us (88%)
  between operations  14.1 us (6%)
  waiting for transfers between devices  8.58 us (4%)
  other arithmetic  2.64 us (1%)
    pallas_call x1, Pallas kernels, run_front(): pl.pallas_call(functools.partial(front_kernel, sizes, heads, experts, own...  76.8 us
    pallas_call x1, Pallas kernels, run_middle(): pl.pallas_call(functools.partial(middle_kernel, sizes, heads, experts, ow...  72.9 us
    pallas_call x1, Pallas kernels, run_last(): pl.pallas_call(functools.partial(last_kernel, sizes, heads, experts, own_...  35.8 us
    pallas_call x1, Pallas kernels, run_expert(): pl.pallas_call(expert_kernel, grid=(hidden // tile,), out_shape=[jax.Shap...  21.3 us
    all_gather x1, waiting for transfers between devices, local(): lax.all_gather(jnp.concatenate([up_weight, down_weight], axis=0), 'ctx',...  8.53 us
  transfers between devices with their start and end apart: 2, of which 1 were waited for; matrix products, arithmetic and copies ran while one was open for 1% of the time, Pallas kernels for 72%

profile of v2, /device:TPU:1, one launch (start us, length us, event | category | flops | bytes accessed | tf_op | source)
XLA Modules:
  0.0 236.4 jit_solution(609543666165820036)
XLA Ops:
  7.2 0.0 all-gather.3.cloned.1.call-start
  7.2 1.9 pad_maximum_fusion
  9.1 0.0 all-gather.3.cloned.1.call-update
  9.2 0.0 all-gather.5.cloned.1.call-start
  9.2 0.7 fusion.7
  9.9 0.6 pad.23.small_in
  10.5 76.8 %run_front.1 = (bf16[8,96,2304]{2,1,0:T(8,128)(2,1)}, bf16[8,16,128]{2,1,0:T(8,128)(2,1)}, bf16[8,96,768]{2,1,0:T(8,128)(2,1)}, bf16[128,768]{1,0:T(8,128)(2,1)}...) custom-call(bf16[96,2304]{1,0:T(8,128)(2,1)} %w_in.1, ...), custom_call_target="tpu_custom_call" | custom-call | flops 60000002048 | bytes 100000000 | tf_op jit(solution)/shard_map/run_front/pallas_call | solution.py:479
  87.3 0.0 all-gather.5.cloned.1.call-update
  87.3 8.5 %all-gather.3.cloned.1.call-done.up_ref.down_ref = bf16[2,3072,768]{2,1,0:T(8,128)(2,1)} async-done(((bf16[2,192,768]{2,1,0:T(8,128)(2,1)}), bf16[2,3072,768]{2,1,0:T(8,128)(2,1)}) %all-gather.3.cloned.1.call-update) | async-done | bytes 9437200 | tf_op jit(solution)/shard_map/all_gather | solution.py:1255
  95.9 21.3 %run_expert.1 = (bf16[512,768]{1,0:T(8,128)(2,1)}, bf16[512,768]{1,0:T(8,128)(2,1)}, f32[8,8,128]{2,1,0:T(8,128)}, bf16[3072,768]{1,0:T(8,128)(2,1)}, bf16[3072,768]{1,0:T(8,128)(2,1)}) custom-call(bf16[512,768]{1,0:T(8,128)(2,1)} %bitcast.33, bf16[512,768]{1,0:T(8,128)(2,1)} %bitcast.34, f32[8,8,128]{2,1,0:T(8,128)} %get-tuple-element.59.gate_ref, ...), custom_call_target="tpu_custom_call" | custom-call | flops 14499999744 | bytes 24000000 | tf_op jit(solution)/shard_map/run_expert/pallas_call | solution.py:575
  117.2 72.9 %run_middle.1 = (bf16[12,192,128]{2,1,0:T(8,128)(2,1)}, bf16[8,64,768]{2,1,0:T(8,128)(2,1)}, bf16[6,16,768]{2,1,0:T(8,128)(2,1)}, bf16[192,2048]{1,0:T(8,128)(2,...) custom-call(bf16[8,64,768]{2,1,0:T(8,128)(2,1)} %bitcast.36, ...), custom_call_target="tpu_custom_call" | custom-call | flops 60000002048 | bytes 100000000 | tf_op jit(solution)/shard_map/run_middle/pallas_call | solution.py:948
  190.1 0.0 all-gather.5.cloned.1.call-done.h_ref
  190.2 35.8 %run_last.1 = (f32[128,768]{1,0:T(8,128)}, bf16[128,768]{1,0:T(8,128)(2,1)}, bf16[12,144,128]{2,1,0:T(8,128)(2,1)}, f32[16,16,128]{2,1,0:T(8,128)}, bf16[6,16,76...) custom-call(bf16[12,192,128]{2,1,0:T(8,128)(2,1)} %get-tuple-element, ...), custom_call_target="tpu_custom_call" | custom-call | flops 4000000000 | bytes 60000000 | tf_op jit(solution)/shard_map/run_last/pallas_call | solution.py:1127
  225.9 3.7 %finish.1 = (bf16[1,128,768]{2,1,0:T(8,128)(2,1)}, f32[1,128,768]{2,1,0:T(8,128)}, f32[1,96]{1,0:T(1,128)}, f32[1,96]{1,0:T(1,128)}, f32[96,2304]{1,0:T(8,128)},...) custom-call(f32[128,768]{1,0:T(8,128)} %get-tuple-element.85.in_ref,, ...), custom_call_target="tpu_custom_call" | custom-call | bytes 8000000 | tf_op jit(solution)/shard_map/finish/pallas_call | solution.py:1210
Async XLA Ops:
  7.2 88.7 %all-gather.3.cloned.1.call-start = ((), (), s32[]{:S(2)}) async-start(), calls=%async_computation | async-start | bytes 10027008 | tf_op jit(solution)/shard_map/all_gather | solution.py:1255
  9.2 181.0 %all-gather.5.cloned.1.call-start = ((), (), s32[]{:S(2)}) async-start(), calls=%async_computation.1 | async-start | bytes 3342336 | tf_op jit(solution)/shard_map/all_gather | solution.py:1296
Sparse Core Ops, SparseCore 0:
  10.7 85.1 all-gather.2
  98.0 57.3 all-gather.4

commit v3 on v2

--- a/solution.py
+++ b/solution.py
@@ -783,8 +783,8 @@
         True, lambda k, h: up_in.at[k, pl.ds(2 * h, 2)], (up_a, up_b, up_c, up_d), sems[18:21]
     )
     downs = RingSum(
-        False,
-        lambda k, h: down_in.at[pl.ds(2 * h, 2), k],
+        True,
+        lambda k, h: down_in.at[k, pl.ds(2 * h, 2)],
         (down_a, down_b, down_c, down_d),
         sems[21:24],
     )
@@ -1028,7 +1028,7 @@
         sems[18:21],
     )
     downs = RingSum(
-        True,
+        False,
         lambda k, h: down_in.at[k, pl.ds(h * part_rows, part_rows)],
         (down_a, down_b, down_c, down_d),
         sems[21:24],

time: 238 us -> 285 us (1.20)
  Pallas kernels: 210 us -> 258 us
    pallas_call x1, Pallas kernels: 72.9 us -> 109 us  [run_middle(): pl.pallas_call(functools.partial(middle_kernel, sizes, heads, experts, ow...]
    pallas_call x1, Pallas kernels: 35.8 us -> 46.7 us  [run_last(): pl.pallas_call(functools.partial(last_kernel, sizes, heads, experts, own_...]
  transfers between devices with their start and end apart: 2 -> 2, of which waited for: 1 -> 1; matrix products, arithmetic and copies ran while one was open for 1% -> 0% of each run, Pallas kernels for 72% -> 73%
where the time goes in v3:
time: 285 us; the launch traced here: 284 us
  Pallas kernels  258 us (91%)
  between operations  14.1 us (5%)
  waiting for transfers between devices  8.58 us (3%)
    pallas_call x1, Pallas kernels, run_middle(): pl.pallas_call(functools.partial(middle_kernel, sizes, heads, experts, ow...  109 us
    pallas_call x1, Pallas kernels, run_front(): pl.pallas_call(functools.partial(front_kernel, sizes, heads, experts, own...  76.8 us
    pallas_call x1, Pallas kernels, run_last(): pl.pallas_call(functools.partial(last_kernel, sizes, heads, experts, own_...  46.7 us
    pallas_call x1, Pallas kernels, run_expert(): pl.pallas_call(expert_kernel, grid=(hidden // tile,), out_shape=[jax.Shap...  21.3 us
    all_gather x1, waiting for transfers between devices, local(): lax.all_gather(jnp.concatenate([up_weight, down_weight], axis=0), 'ctx',...  8.53 us
  transfers between devices with their start and end apart: 2, of which 1 were waited for; matrix products, arithmetic and copies ran while one was open for 0% of the time, Pallas kernels for 73%

profile of v3, /device:TPU:1, one launch (start us, length us, event | category | flops | bytes accessed | tf_op | source)
XLA Modules:
  0.0 283.9 jit_solution(6944005096441284736)
XLA Ops:
  7.2 0.0 all-gather.3.cloned.1.call-start
  7.2 1.9 pad_maximum_fusion
  9.1 0.0 all-gather.3.cloned.1.call-update
  9.2 0.0 all-gather.5.cloned.1.call-start
  9.2 0.7 fusion.7
  9.9 0.6 pad.23.small_in
  10.5 76.8 %run_front.1 = (bf16[8,96,2304]{2,1,0:T(8,128)(2,1)}, bf16[8,16,128]{2,1,0:T(8,128)(2,1)}, bf16[8,96,768]{2,1,0:T(8,128)(2,1)}, bf16[128,768]{1,0:T(8,128)(2,1)}...) custom-call(bf16[96,2304]{1,0:T(8,128)(2,1)} %w_in.1, ...), custom_call_target="tpu_custom_call" | custom-call | flops 60000002048 | bytes 100000000 | tf_op jit(solution)/shard_map/run_front/pallas_call | solution.py:479
  87.3 0.0 all-gather.5.cloned.1.call-update
  87.3 8.5 %all-gather.3.cloned.1.call-done.up_ref.down_ref = bf16[2,3072,768]{2,1,0:T(8,128)(2,1)} async-done(((bf16[2,192,768]{2,1,0:T(8,128)(2,1)}), bf16[2,3072,768]{2,1,0:T(8,128)(2,1)}) %all-gather.3.cloned.1.call-update) | async-done | bytes 9437200 | tf_op jit(solution)/shard_map/all_gather | solution.py:1255
  95.9 21.3 %run_expert.1 = (bf16[512,768]{1,0:T(8,128)(2,1)}, bf16[512,768]{1,0:T(8,128)(2,1)}, f32[8,8,128]{2,1,0:T(8,128)}, bf16[3072,768]{1,0:T(8,128)(2,1)}, bf16[3072,768]{1,0:T(8,128)(2,1)}) custom-call(bf16[512,768]{1,0:T(8,128)(2,1)} %bitcast.33, bf16[512,768]{1,0:T(8,128)(2,1)} %bitcast.34, f32[8,8,128]{2,1,0:T(8,128)} %get-tuple-element.59.gate_ref, ...), custom_call_target="tpu_custom_call" | custom-call | flops 14499999744 | bytes 24000000 | tf_op jit(solution)/shard_map/run_expert/pallas_call | solution.py:575
  117.2 109.5 %run_middle.1 = (bf16[12,192,128]{2,1,0:T(8,128)(2,1)}, bf16[8,64,768]{2,1,0:T(8,128)(2,1)}, bf16[6,16,768]{2,1,0:T(8,128)(2,1)}, bf16[192,2048]{1,0:T(8,128)(2,...) custom-call(bf16[8,64,768]{2,1,0:T(8,128)(2,1)} %bitcast.36, ...), custom_call_target="tpu_custom_call" | custom-call | flops 60000002048 | bytes 100000000 | tf_op jit(solution)/shard_map/run_middle/pallas_call | solution.py:948
  226.7 0.0 all-gather.5.cloned.1.call-done.h_ref
  226.7 46.7 %run_last.1 = (f32[128,768]{1,0:T(8,128)}, bf16[128,768]{1,0:T(8,128)(2,1)}, bf16[12,144,128]{2,1,0:T(8,128)(2,1)}, f32[16,16,128]{2,1,0:T(8,128)}, bf16[6,16,76...) custom-call(bf16[12,192,128]{2,1,0:T(8,128)(2,1)} %get-tuple-element, ...), custom_call_target="tpu_custom_call" | custom-call | flops 4000000000 | bytes 60000000 | tf_op jit(solution)/shard_map/run_last/pallas_call | solution.py:1127
  273.4 3.7 %finish.1 = (bf16[1,128,768]{2,1,0:T(8,128)(2,1)}, f32[1,128,768]{2,1,0:T(8,128)}, f32[1,96]{1,0:T(1,128)}, f32[1,96]{1,0:T(1,128)}, f32[96,2304]{1,0:T(8,128)},...) custom-call(f32[128,768]{1,0:T(8,128)} %get-tuple-element.85.in_ref,, ...), custom_call_target="tpu_custom_call" | custom-call | bytes 8000000 | tf_op jit(solution)/shard_map/finish/pallas_call | solution.py:1210
Async XLA Ops:
  7.2 88.7 %all-gather.3.cloned.1.call-start = ((), (), s32[]{:S(2)}) async-start(), calls=%async_computation | async-start | bytes 10027008 | tf_op jit(solution)/shard_map/all_gather | solution.py:1255
  9.2 217.5 %all-gather.5.cloned.1.call-start = ((), (), s32[]{:S(2)}) async-start(), calls=%async_computation.1 | async-start | bytes 3342336 | tf_op jit(solution)/shard_map/all_gather | solution.py:1296
Sparse Core Ops, SparseCore 0:
  10.7 85.1 all-gather.2
  98.0 59.4 all-gather.4
